TPU v7x, 32 devices: a whole 2x2x4 slice. The times are simulated.
32 devices in a mesh: gx: 4 (over y, x), gy: 8 (over z, core).
Axes of the slice: x: 2, y: 2, z: 4, core: 2. Of those that a mesh axis runs over, the one named last changes fastest.
Arguments:
- probes: bfloat16 [8, 64, 32, 128], P('gx', 'gy'), may hold values from -6 to 6
- leaf_basis: bfloat16 [128, 64], replicated, may hold values from -0.5 to 0.5
- up_transfer: bfloat16 [7, 4, 64, 64], replicated, may hold values from -0.375 to 0.375
- down_transfer: bfloat16 [7, 4, 64, 64], replicated, may hold values from -0.75 to 0.75
- coupling: bfloat16 [8, 40, 64, 64], replicated, may hold values from -0.15625 to 0.15625
- far_ids: int32 [8, 4, 27], replicated, may hold values from 0 to 39
Outputs:
- product: bfloat16 [8, 64, 32, 128], P('gx', 'gy')
Inputs may be any that keep to these rules, and one draw needn't show every extreme that they name: `far_ids`: each entry picks one of the 40 coupling matrices of its level.
All inputs are finite; a program needn't handle non-finite values.
Results may differ from a plain program's by a relative error of at most 0.012.
Values may be sent and summed in bfloat16 or wider, within the bound.
A program may use at most 128 MiB of HBM per device.

v0:
```python
import jax
import jax.numpy as jnp
from jax import lax
from jax.sharding import PartitionSpec as P

LEAF_ROWS = 8
LEAF_COLS = 16


length_scale = 1.5


def shifted(block, axis, distance):
    devices = range(lax.axis_size(axis))
    route = [(i - distance, i) for i in devices if i - distance in devices]
    return lax.ppermute(block, axis, route)


def with_halo(value, sides, width):
    for axis, dim in sides:
        count, length = (lax.axis_size(axis), value.shape[dim])
        up = [(i, (i + 1) % count) for i in range(count - 1)]
        down = [(j, i) for i, j in up]
        last = lax.slice_in_dim(value, length - width, length, axis=dim)
        leading = lax.slice_in_dim(value, 0, width, axis=dim)
        before = lax.ppermute(last, axis, up)
        after = lax.ppermute(leading, axis, down)
        value = jnp.concatenate([before, value, after], axis=dim)
    return value


def slot_offsets(type_row, type_col):
    offsets = []
    for off_row in range(-2 - type_row, 4 - type_row):
        for off_col in range(-2 - type_col, 4 - type_col):
            if max(abs(off_row), abs(off_col)) > 1:
                offsets.append((off_row, off_col))
    return offsets


def kernel_tables(rows_leaf, cols_leaf):
    points = jnp.arange(rows_leaf * cols_leaf, dtype=jnp.int32)
    point_row = (points // cols_leaf).astype(jnp.float32)
    point_col = (points % cols_leaf).astype(jnp.float32)
    tables = []
    for off_row in (-1, 0, 1):
        for off_col in (-1, 0, 1):
            apart_row = point_row[:, None] + off_row * rows_leaf - point_row[None, :]
            apart_col = point_col[:, None] + off_col * cols_leaf - point_col[None, :]
            scaled = jnp.sqrt(3.0 * (apart_row * apart_row + apart_col * apart_col)) / length_scale
            tables.append(((1.0 + scaled) * jnp.exp(-scaled)).astype(jnp.bfloat16))
    return jnp.stack(tables)


def along_rows(values, offset):
    return shifted(values, "gx", offset)


def along_cols(values, offset):
    return shifted(values, "gy", offset)


def tile_level(tile_size, height):
    nodes_dev = max(1, tile_size >> height)
    ascent = max(0, height - (tile_size.bit_length() - 1))
    return (nodes_dev, ascent)


def widen_dim(values, axis_dim, count_dev, nodes_dev, ascent, shifter):
    stride_dev = 1 << ascent
    reach_dev = 3 if nodes_dev == 1 else (nodes_dev + 2) // nodes_dev
    pieces = []
    for distance in range(reach_dev, 0, -1):
        moved = distance * stride_dev
        pieces.append(shifter(values, moved) if moved < count_dev else jnp.zeros_like(values))
    pieces.append(values)
    for distance in range(1, reach_dev + 1):
        moved = distance * stride_dev
        pieces.append(shifter(values, -moved) if moved < count_dev else jnp.zeros_like(values))
    joined = jnp.concatenate(pieces, axis=axis_dim)
    return lax.slice_in_dim(
        joined, reach_dev * nodes_dev - 3, reach_dev * nodes_dev + nodes_dev + 3, axis=axis_dim
    )


def join_types(first_part, second_part, axis_dim, nodes_dev, bit_value):
    if nodes_dev > 1:
        stacked = jnp.stack([first_part, second_part], axis=axis_dim + 1)
        target_shape = list(first_part.shape)
        target_shape[axis_dim] = 2 * target_shape[axis_dim]
        return stacked.reshape(target_shape)
    return jnp.where(bit_value == 0, first_part, second_part)


def far_terms(widened, coupling_level, ids_level, nodes_row, nodes_col, bit_row, bit_col):
    count_p, rank_size = (widened.shape[2], widened.shape[3])
    count_row = max(1, nodes_row // 2)
    count_col = max(1, nodes_col // 2)
    results = []
    for type_row in (0, 1):
        row_parts = []
        for type_col in (0, 1):
            first_row = type_row if nodes_row > 1 else 0
            first_col = type_col if nodes_col > 1 else 0
            offsets = slot_offsets(type_row, type_col)
            chosen = jnp.take(coupling_level, ids_level[2 * type_row + type_col], axis=0)
            chosen = chosen.reshape(len(offsets) * rank_size, rank_size)
            pieces = []
            for off_row, off_col in offsets:
                start_row = first_row + 3 + off_row
                start_col = first_col + 3 + off_col
                pieces.append(
                    lax.slice(
                        widened,
                        (start_row, start_col, 0, 0),
                        (
                            start_row + 2 * count_row - 1,
                            start_col + 2 * count_col - 1,
                            count_p,
                            rank_size,
                        ),
                        (2, 2, 1, 1),
                    )
                )
            stacked = jnp.concatenate(pieces, axis=3)
            summed = jnp.einsum(
                "ijpk,kq->ijpq", stacked, chosen, preferred_element_type=jnp.float32
            )
            row_parts.append(summed)
        results.append(join_types(row_parts[0], row_parts[1], 1, nodes_col, bit_col))
    return join_types(results[0], results[1], 0, nodes_row, bit_row)


def gather_children(values, axis_dim, nodes_dev, ascent, count_dev, shifter):
    if nodes_dev > 1:
        target_shape = list(values.shape)
        target_shape[axis_dim : axis_dim + 1] = [nodes_dev // 2, 2]
        return values.reshape(target_shape)
    if 1 << ascent >= count_dev:
        return jnp.stack([values, jnp.zeros_like(values)], axis=axis_dim + 1)
    partner = shifter(values, -(1 << ascent))
    return jnp.stack([values, partner], axis=axis_dim + 1)


def spread_parent(values, nodes_dev, ascent, count_dev, device_index, shifter):
    if nodes_dev > 1 or 1 << ascent >= count_dev:
        return values
    own_bit = device_index // (1 << ascent) % 2
    return jnp.where(own_bit == 1, shifter(values, 1 << ascent), values)


def pick_child(spread, axis_dim, nodes_dev, bit_value):
    if nodes_dev > 1:
        return spread
    return jnp.where(
        bit_value == 0,
        lax.slice_in_dim(spread, 0, 1, axis=axis_dim + 1),
        lax.slice_in_dim(spread, 1, 2, axis=axis_dim + 1),
    )


def shards(probes, leaf_basis, up_transfer, down_transfer, coupling, far_ids):
    tile_x, tile_y, count_p, leaf_size = probes.shape
    rank_size = leaf_basis.shape[1]
    levels = coupling.shape[0]
    rows_count = lax.axis_size("gx")
    cols_count = lax.axis_size("gy")
    row_index = lax.axis_index("gx")
    col_index = lax.axis_index("gy")
    padded = with_halo(probes, (("gx", 0), ("gy", 1)), 1)
    tables = kernel_tables(LEAF_ROWS, LEAF_COLS).reshape(9 * leaf_size, leaf_size)
    near_pieces = []
    for off_row in (-1, 0, 1):
        for off_col in (-1, 0, 1):
            near_pieces.append(
                padded[1 + off_row : 1 + off_row + tile_x, 1 + off_col : 1 + off_col + tile_y]
            )
    near_stack = jnp.concatenate(near_pieces, axis=3).reshape(-1, 9 * leaf_size)
    near_sum = jnp.dot(near_stack, tables, preferred_element_type=jnp.float32)
    first = jnp.dot(probes.reshape(-1, leaf_size), leaf_basis, preferred_element_type=jnp.float32)
    ladder = [first.reshape(tile_x, tile_y, count_p, rank_size).astype(jnp.bfloat16)]
    for height in range(levels - 1):
        nodes_row, ascent_row = tile_level(tile_x, height)
        nodes_col, ascent_col = tile_level(tile_y, height)
        grouped = gather_children(ladder[-1], 0, nodes_row, ascent_row, rows_count, along_rows)
        grouped = gather_children(grouped, 2, nodes_col, ascent_col, cols_count, along_cols)
        parent_coef = jnp.einsum(
            "iajbpr,abrq->ijpq",
            grouped,
            up_transfer[height].reshape(2, 2, rank_size, rank_size),
            preferred_element_type=jnp.float32,
        )
        ladder.append(parent_coef.astype(jnp.bfloat16))
    carried = None
    for height in reversed(range(levels)):
        nodes_row, ascent_row = tile_level(tile_x, height)
        nodes_col, ascent_col = tile_level(tile_y, height)
        bit_row = row_index // (1 << ascent_row) % 2
        bit_col = col_index // (1 << ascent_col) % 2
        widened = widen_dim(ladder[height], 0, rows_count, nodes_row, ascent_row, along_rows)
        widened = widen_dim(widened, 1, cols_count, nodes_col, ascent_col, along_cols)
        summed = far_terms(
            widened, coupling[height], far_ids[height], nodes_row, nodes_col, bit_row, bit_col
        )
        if carried is not None:
            parent = carried
            parent = spread_parent(parent, nodes_row, ascent_row, rows_count, row_index, along_rows)
            parent = spread_parent(parent, nodes_col, ascent_col, cols_count, col_index, along_cols)
            spread = jnp.einsum(
                "ijpr,abrq->iajbpq",
                parent,
                down_transfer[height].reshape(2, 2, rank_size, rank_size),
                preferred_element_type=jnp.float32,
            )
            spread = pick_child(spread, 0, nodes_row, bit_row)
            spread = pick_child(spread, 2, nodes_col, bit_col)
            summed = summed + spread.reshape(summed.shape)
        carried = summed.astype(jnp.bfloat16)
    far_sum = jnp.einsum(
        "nr,qr->nq", carried.reshape(-1, rank_size), leaf_basis, preferred_element_type=jnp.float32
    )
    return (near_sum + far_sum).reshape(tile_x, tile_y, count_p, leaf_size).astype(jnp.bfloat16)


def solution(mesh):
    in_specs = (P("gx", "gy", None, None), P(), P(), P(), P(), P())
    out_specs = P("gx", "gy", None, None)
    return jax.shard_map(shards, mesh=mesh, in_specs=in_specs, out_specs=out_specs, check_vma=False)
```

profile of v0, /device:TPU:1, one launch (start us, length us, event | category | flops | bytes accessed | tf_op | source)
XLA Modules:
  0.0 350.7 jit_solution(6869005028007295454)
XLA Ops:
  0.0 1.8 fusion.136
  1.8 1.7 convolution_convert_fusion
  3.5 1.7 fusion.1
  6.5 7.0 %collective-permute-start.10 = (bf16[1,4,32,64]{3,2,1,0:T(8,128)(2,1)}, bf16[1,4,32,64]{3,2,1,0:T(8,128)(2,1)}, u32[]{:S(2)}, u32[]{:S(2)}) collective-permute-start(bf16[1,4,32,64]{3,2,1,0:T(8,128)(2,1)} %bitcast.34), channel_id=1, source_target_pairs={{0,24},{1,25},{2,26},{3,27},{4,28},{5,29},{6,30},{7,31}} | collective-permute-start | bytes 49160 | tf_op jit(solution)/shard_map/ppermute | solution.py:16
  13.5 1.9 collective-permute-start.11
  15.4 2.2 collective-permute-start.12
  19.8 5.3 %slice_bitcast_fusion.7 = (bf16[40,64,64]{2,1,0:T(8,128)(2,1)S(1)}, bf16[40,64,64]{2,1,0:T(8,128)(2,1)S(1)}, bf16[40,64,64]{2,1,0:T(8,128)(2,1)S(1)}, bf16[40,64...) fusion(bf16[8,40,64,64]{3,2,1,0:T(8,128)(2,1)} %param.12), kind=kLoop, calls=%fused_computation.104 | loop fusion | bytes 5242880 | tf_op jit(solution)/shard_map/squeeze | solution.py:203
  25.1 2.5 gather_fusion.25
  27.5 2.5 gather_fusion.24
  30.0 2.1 broadcast_select_fusion.6
  32.9 2.5 gather_fusion.27
  35.4 2.5 gather_fusion.26
  37.8 2.1 broadcast_select_fusion.4
  40.7 2.5 gather_fusion.29
  43.2 2.5 gather_fusion.28
  45.7 2.1 broadcast_select_fusion.2
  48.6 2.5 gather_fusion.30
  53.0 2.5 gather_fusion.31
  55.4 1.9 broadcast_select_fusion
  57.3 1.9 convolution_select_fusion.1
  59.2 2.0 convolution_bitcast_fusion.6
  64.4 4.2 %collective-permute-start.38 = (bf16[1,1,32,64]{3,2,1,0:T(8,128)(2,1)S(1)}, bf16[1,1,32,64]{3,2,1,0:T(8,128)(2,1)S(1)}, u32[]{:S(2)}, u32[]{:S(2)}) collective-permute-start(bf16[1,1,32,64]{3,2,1,0:T(8,128)(2,1)S(1)} %fusion.23), channel_id=1, source_target_pairs={{0,4},{1,5},{2,6},{3,7},{8,12},{9,13},{10,14},{11,15},{16,20},{17,... | collective-permute-start | bytes 12296 | tf_op jit(solution)/shard_map/ppermute | solution.py:16
  73.0 2.5 gather_fusion.15
  75.5 2.5 gather_fusion.13
  78.6 2.5 gather_fusion.14
  81.1 2.5 gather_fusion.12
  134.0 4.0 %collective-permute-start.4 = (bf16[2,8,32,64]{3,2,1,0:T(8,128)(2,1)}, bf16[2,8,32,64]{3,2,1,0:T(8,128)(2,1)}, u32[]{:S(2)}, u32[]{:S(2)}) collective-permute-start(bf16[2,8,32,64]{3,2,1,0:T(8,128)(2,1)} %convolution_convert_fusion), channel_id=1, source_target_pairs={{0,16},{8,24},{1,17},{9,25},{2,18},{10,26},{3,19},{11,27},{4,20},{... | collective-permute-start | bytes 196616 | tf_op jit(solution)/shard_map/ppermute | solution.py:16
  138.8 4.4 %collective-permute-start.5 = (bf16[2,8,32,64]{3,2,1,0:T(8,128)(2,1)}, bf16[2,8,32,64]{3,2,1,0:T(8,128)(2,1)}, u32[]{:S(2)}, u32[]{:S(2)}) collective-permute-start(bf16[2,8,32,64]{3,2,1,0:T(8,128)(2,1)} %convolution_convert_fusion), channel_id=1, source_target_pairs={{0,8},{8,16},{16,24},{1,9},{9,17},{17,25},{2,10},{10,18},{18,26},{... | collective-permute-start | bytes 196616 | tf_op jit(solution)/shard_map/ppermute | solution.py:16
  150.5 3.8 %collective-permute-done.19 = bf16[1,2,32,64]{3,2,1,0:T(8,128)(2,1)S(1)} collective-permute-done((bf16[1,2,32,64]{3,2,1,0:T(8,128)(2,1)S(1)}, bf16[1,2,32,64]{3,2,1,0:T(8,128)(2,1)S(1)}, u32[]{:S(2)}, u32[]{:S(2)}) %collective-permute-start.19) | collective-permute-done | bytes 8224 | tf_op jit(solution)/shard_map/ppermute | solution.py:16
  154.3 1.6 collective-permute-start.18
  157.3 5.7 %collective-permute-start.28 = (bf16[1,2,1,32,64]{4,3,2,1,0:T(8,128)(2,1)S(1)}, bf16[1,2,1,32,64]{4,3,2,1,0:T(8,128)(2,1)S(1)}, u32[]{:S(2)}, u32[]{:S(2)}) collective-permute-start(bf16[1,2,1,32,64]{4,3,2,1,0:T(8,128)(2,1)S(1)} %get-tuple-element.333), channel_id=1, source_target_pairs={{1,0},{2,1},{3,2},{4,3},{5,4},{6,5},{7,6},{9,8},{10,9},{11,10},{12... | collective-permute-start | bytes 24584 | tf_op jit(solution)/shard_map/ppermute | solution.py:16
  170.1 3.0 collective-permute-done.35
  173.1 3.0 collective-permute-start.27
  178.2 3.7 %collective-permute-start.22 = (bf16[7,1,32,64]{3,2,1,0:T(8,128)(2,1)}, bf16[7,1,32,64]{3,2,1,0:T(8,128)(2,1)S(1)}, u32[]{:S(2)}, u32[]{:S(2)}) collective-permute-start(bf16[7,1,32,64]{3,2,1,0:T(8,128)(2,1)} %constant_dynamic-update-slice_fusion.30), channel_id=1, source_target_pairs={{0,2},{1,3},{2,4},{3,5},{4,6},{5,7},{8,10},{9,11},{10,12},{11,13},... | collective-permute-start | bytes 86024 | tf_op jit(solution)/shard_map/ppermute | solution.py:16
  183.4 4.2 %collective-permute-start.23 = (bf16[7,1,32,64]{3,2,1,0:T(8,128)(2,1)}, bf16[7,1,32,64]{3,2,1,0:T(8,128)(2,1)S(1)}, u32[]{:S(2)}, u32[]{:S(2)}) collective-permute-start(bf16[7,1,32,64]{3,2,1,0:T(8,128)(2,1)} %constant_dynamic-update-slice_fusion.30), channel_id=1, source_target_pairs={{0,1},{1,2},{2,3},{3,4},{4,5},{5,6},{6,7},{8,9},{9,10},{10,11},{11... | collective-permute-start | bytes 86024 | tf_op jit(solution)/shard_map/ppermute | solution.py:16
  189.2 1.9 collective-permute-start.24
  191.8 3.7 %collective-permute-done.24 = bf16[7,1,32,64]{3,2,1,0:T(8,128)(2,1)S(1)} collective-permute-done((bf16[7,1,32,64]{3,2,1,0:T(8,128)(2,1)}, bf16[7,1,32,64]{3,2,1,0:T(8,128)(2,1)S(1)}, u32[]{:S(2)}, u32[]{:S(2)}) %collective-permute-start.24) | collective-permute-done | bytes 28704 | tf_op jit(solution)/shard_map/ppermute | solution.py:16
  197.3 3.7 %collective-permute-done.25 = bf16[7,1,32,64]{3,2,1,0:T(8,128)(2,1)S(1)} collective-permute-done((bf16[7,1,32,64]{3,2,1,0:T(8,128)(2,1)}, bf16[7,1,32,64]{3,2,1,0:T(8,128)(2,1)S(1)}, u32[]{:S(2)}, u32[]{:S(2)}) %collective-permute-start.25) | collective-permute-done | bytes 28704 | tf_op jit(solution)/shard_map/ppermute | solution.py:16
  203.3 1.8 fusion.60
  205.1 2.7 collective-permute-done.26
  207.8 4.6 %collective-permute-start.34 = (bf16[7,1,32,64]{3,2,1,0:T(8,128)(2,1)}, bf16[7,1,32,64]{3,2,1,0:T(8,128)(2,1)}, u32[]{:S(2)}, u32[]{:S(2)}) collective-permute-start(bf16[7,1,32,64]{3,2,1,0:T(8,128)(2,1)} %constant_dynamic-update-slice_fusion.35), channel_id=1, source_target_pairs={{0,6},{1,7},{8,14},{9,15},{16,22},{17,23},{24,30},{25,31}} | collective-permute-start | bytes 86024 | tf_op jit(solution)/shard_map/ppermute | solution.py:16
  214.8 1.8 convolution_select_fusion.8
  217.5 1.8 fusion.63
  223.7 1.7 collective-permute-start.30
  228.9 4.9 %collective-permute-done.31 = bf16[7,1,32,64]{3,2,1,0:T(8,128)(2,1)S(1)} collective-permute-done((bf16[7,1,32,64]{3,2,1,0:T(8,128)(2,1)}, bf16[7,1,32,64]{3,2,1,0:T(8,128)(2,1)S(1)}, u32[]{:S(2)}, u32[]{:S(2)}) %collective-permute-start.31) | collective-permute-done | bytes 28704 | tf_op jit(solution)/shard_map/ppermute | solution.py:16
  235.6 4.1 %collective-permute-done.32 = bf16[7,1,32,64]{3,2,1,0:T(8,128)(2,1)S(1)} collective-permute-done((bf16[7,1,32,64]{3,2,1,0:T(8,128)(2,1)}, bf16[7,1,32,64]{3,2,1,0:T(8,128)(2,1)S(1)}, u32[]{:S(2)}, u32[]{:S(2)}) %collective-permute-start.32) | collective-permute-done | bytes 28704 | tf_op jit(solution)/shard_map/ppermute | solution.py:16
  242.5 1.8 fusion.54
  244.3 2.5 collective-permute-done.33
  246.8 4.3 %collective-permute-start = (bf16[1,8,32,128]{3,2,1,0:T(8,128)(2,1)}, bf16[1,8,32,128]{3,2,1,0:T(8,128)(2,1)S(1)}, u32[]{:S(2)}, u32[]{:S(2)}) collective-permute-start(bf16[1,8,32,128]{3,2,1,0:T(8,128)(2,1)} %get-tuple-element.161), channel_id=1, source_target_pairs={{0,8},{8,16},{16,24},{1,9},{9,17},{17,25},{2,10},{10,18},{18,26},{... | collective-permute-start | bytes 196616 | tf_op jit(solution)/shard_map/ppermute | solution.py:26
  253.5 1.8 convolution_select_fusion.6
  260.9 7.8 %collective-permute-start.17 = (bf16[7,4,32,64]{3,2,1,0:T(8,128)(2,1)}, bf16[7,4,32,64]{3,2,1,0:T(8,128)(2,1)}, u32[]{:S(2)}, u32[]{:S(2)}) collective-permute-start(bf16[7,4,32,64]{3,2,1,0:T(8,128)(2,1)} %copy-done.52), channel_id=1, source_target_pairs={{1,0},{2,1},{3,2},{4,3},{5,4},{6,5},{7,6},{9,8},{10,9},{11,10},{12... | collective-permute-start | bytes 344072 | tf_op jit(solution)/shard_map/ppermute | solution.py:16
  270.6 1.9 collective-permute-start.16
  272.6 3.2 collective-permute-start.36
  278.9 4.6 %collective-permute-done.37 = bf16[7,1,32,64]{3,2,1,0:T(8,128)(2,1)S(1)} collective-permute-done((bf16[7,1,32,64]{3,2,1,0:T(8,128)(2,1)S(1)}, bf16[7,1,32,64]{3,2,1,0:T(8,128)(2,1)S(1)}, u32[]{:S(2)}, u32[]{:S(2)}) %collective-permute-start.37) | collective-permute-done | bytes 28704 | tf_op jit(solution)/shard_map/ppermute | solution.py:16
  283.5 4.6 %collective-permute-start.20 = (bf16[7,2,32,64]{3,2,1,0:T(8,128)(2,1)}, bf16[7,2,32,64]{3,2,1,0:T(8,128)(2,1)}, u32[]{:S(2)}, u32[]{:S(2)}) collective-permute-start(bf16[7,2,32,64]{3,2,1,0:T(8,128)(2,1)} %constant_dynamic-update-slice_fusion.25), channel_id=1, source_target_pairs={{0,1},{1,2},{2,3},{3,4},{4,5},{5,6},{6,7},{8,9},{9,10},{10,11},{11... | collective-permute-start | bytes 172040 | tf_op jit(solution)/shard_map/ppermute | solution.py:16
  299.1 3.3 collective-permute-start.21
  302.8 3.8 %collective-permute-start.40 = (bf16[1,1,32,64]{3,2,1,0:T(8,128)(2,1)S(1)}, bf16[1,1,32,64]{3,2,1,0:T(8,128)(2,1)S(1)}, u32[]{:S(2)}, u32[]{:S(2)}) collective-permute-start(bf16[1,1,32,64]{3,2,1,0:T(8,128)(2,1)S(1)} %fusion.25), channel_id=1, source_target_pairs={{0,1},{1,2},{2,3},{3,4},{4,5},{5,6},{6,7},{8,9},{9,10},{10,11},{11... | collective-permute-start | bytes 12296 | tf_op jit(solution)/shard_map/ppermute | solution.py:16
  307.5 1.9 collective-permute-start.9
  309.8 4.0 %collective-permute-start.8 = (bf16[8,8,32,64]{3,2,1,0:T(8,128)(2,1)S(1)}, bf16[8,8,32,64]{3,2,1,0:T(8,128)(2,1)}, u32[]{:S(2)}, u32[]{:S(2)}) collective-permute-start(bf16[8,8,32,64]{3,2,1,0:T(8,128)(2,1)S(1)} %slice.1838), channel_id=1, source_target_pairs={{0,1},{1,2},{2,3},{3,4},{4,5},{5,6},{6,7},{8,9},{9,10},{10,11},{11... | collective-permute-start | bytes 786440 | tf_op jit(solution)/shard_map/ppermute | solution.py:16
  314.8 4.8 %collective-permute-start.41 = (bf16[1,1,32,64]{3,2,1,0:T(8,128)(2,1)S(1)}, bf16[1,1,32,64]{3,2,1,0:T(8,128)(2,1)S(1)}, u32[]{:S(2)}, u32[]{:S(2)}) collective-permute-start(bf16[1,1,32,64]{3,2,1,0:T(8,128)(2,1)S(1)} %fusion.26), channel_id=1, source_target_pairs={{0,16},{8,24},{1,17},{9,25},{2,18},{10,26},{3,19},{11,27},{4,20},{... | collective-permute-start | bytes 12296 | tf_op jit(solution)/shard_map/ppermute | solution.py:16
  321.2 4.0 %collective-permute-start.42 = (bf16[1,2,32,64]{3,2,1,0:T(8,128)(2,1)S(1)}, bf16[1,2,32,64]{3,2,1,0:T(8,128)(2,1)S(1)}, u32[]{:S(2)}, u32[]{:S(2)}) collective-permute-start(bf16[1,2,32,64]{3,2,1,0:T(8,128)(2,1)S(1)} %fusion.90), channel_id=1, source_target_pairs={{0,8},{8,16},{16,24},{1,9},{9,17},{17,25},{2,10},{10,18},{18,26},{... | collective-permute-start | bytes 24584 | tf_op jit(solution)/shard_map/ppermute | solution.py:16
  326.0 3.5 %collective-permute-start.2 = (bf16[4,1,32,128]{3,2,1,0:T(8,128)(2,1)S(1)}, bf16[4,1,32,128]{3,2,1,0:T(8,128)(2,1)S(1)}, u32[]{:S(2)}, u32[]{:S(2)}) collective-permute-start(bf16[4,1,32,128]{3,2,1,0:T(8,128)(2,1)S(1)} %get-tuple-element.159), channel_id=1, source_target_pairs={{0,1},{1,2},{2,3},{3,4},{4,5},{5,6},{6,7},{8,9},{9,10},{10,11},{11... | collective-permute-start | bytes 98312 | tf_op jit(solution)/shard_map/ppermute | solution.py:26
  330.6 1.9 collective-permute-start.3
  332.6 3.8 %collective-permute-done.3 = bf16[4,1,32,128]{3,2,1,0:T(8,128)(2,1)S(1)} collective-permute-done((bf16[4,1,32,128]{3,2,1,0:T(8,128)(2,1)S(1)}, bf16[4,1,32,128]{3,2,1,0:T(8,128)(2,1)S(1)}, u32[]{:S(2)}, u32[]{:S(2)}) %collective-permute-start.3) | collective-permute-done | bytes 32800 | tf_op jit(solution)/shard_map/ppermute | solution.py:27
  (545 shorter events, 151.2 us)
Async XLA Ops:
  0.0 17.6 %copy-start.87 = (s32[8,4,27]{2,1,0:T(4,128)S(1)}, s32[8,4,27]{2,1,0:T(4,128)}, u32[]{:S(2)}) copy-start(s32[8,4,27]{2,1,0:T(4,128)} %param.13) | copy-start | bytes 10372
  0.0 19.0 %copy-start.47 = (bf16[7,4,64,64]{3,2,1,0:T(8,128)(2,1)S(1)}, bf16[7,4,64,64]{3,2,1,0:T(8,128)(2,1)}, u32[]{:S(2)}) copy-start(bf16[7,4,64,64]{3,2,1,0:T(8,128)(2,1)} %param.11) | copy-start | bytes 688132
  5.2 139.4 %collective-permute-start.13 = (bf16[1,4,32,64]{3,2,1,0:T(8,128)(2,1)}, bf16[1,4,32,64]{3,2,1,0:T(8,128)(2,1)}, u32[]{:S(2)}, u32[]{:S(2)}) collective-permute-start(bf16[1,4,32,64]{3,2,1,0:T(8,128)(2,1)} %bitcast.34), channel_id=1, source_target_pairs={{8,0},{16,8},{24,16},{9,1},{17,9},{25,17},{10,2},{18,10},{26,18},{... | collective-permute-start | bytes 49160 | tf_op jit(solution)/shard_map/ppermute | solution.py:16
  6.5 125.4 %collective-permute-start.10 = (bf16[1,4,32,64]{3,2,1,0:T(8,128)(2,1)}, bf16[1,4,32,64]{3,2,1,0:T(8,128)(2,1)}, u32[]{:S(2)}, u32[]{:S(2)}) collective-permute-start(bf16[1,4,32,64]{3,2,1,0:T(8,128)(2,1)} %bitcast.34), channel_id=1, source_target_pairs={{0,24},{1,25},{2,26},{3,27},{4,28},{5,29},{6,30},{7,31}} | collective-permute-start | bytes 49160 | tf_op jit(solution)/shard_map/ppermute | solution.py:16
  13.5 120.5 %collective-permute-start.11 = (bf16[1,4,32,64]{3,2,1,0:T(8,128)(2,1)}, bf16[1,4,32,64]{3,2,1,0:T(8,128)(2,1)}, u32[]{:S(2)}, u32[]{:S(2)}) collective-permute-start(bf16[1,4,32,64]{3,2,1,0:T(8,128)(2,1)} %bitcast.34), channel_id=1, source_target_pairs={{0,16},{8,24},{1,17},{9,25},{2,18},{10,26},{3,19},{11,27},{4,20},{... | collective-permute-start | bytes 49160 | tf_op jit(solution)/shard_map/ppermute | solution.py:16
  15.4 123.4 %collective-permute-start.12 = (bf16[1,4,32,64]{3,2,1,0:T(8,128)(2,1)}, bf16[1,4,32,64]{3,2,1,0:T(8,128)(2,1)}, u32[]{:S(2)}, u32[]{:S(2)}) collective-permute-start(bf16[1,4,32,64]{3,2,1,0:T(8,128)(2,1)} %bitcast.34), channel_id=1, source_target_pairs={{0,8},{8,16},{16,24},{1,9},{9,17},{17,25},{2,10},{10,18},{18,26},{... | collective-permute-start | bytes 49160 | tf_op jit(solution)/shard_map/ppermute | solution.py:16
  57.3 13.7 %copy-start.1 = (bf16[2,8,32,128]{3,2,1,0:T(8,128)(2,1)S(1)}, bf16[2,8,32,128]{3,2,1,0:T(8,128)(2,1)}, u32[]{:S(2)}) copy-start(bf16[2,8,32,128]{3,2,1,0:T(8,128)(2,1)} %param.8) | copy-start | bytes 393220
  64.4 14.2 %copy-start.121 = (s32[27]{0:T(128)S(1)}, s32[27]{0:T(128)}, u32[]{:S(2)}) copy-start(s32[27]{0:T(128)} %get-tuple-element.301) | copy-start | bytes 328
  64.4 14.2 %copy-start.122 = (s32[27]{0:T(128)S(1)}, s32[27]{0:T(128)}, u32[]{:S(2)}) copy-start(s32[27]{0:T(128)} %get-tuple-element.305) | copy-start | bytes 328
  64.4 65.4 %collective-permute-start.38 = (bf16[1,1,32,64]{3,2,1,0:T(8,128)(2,1)S(1)}, bf16[1,1,32,64]{3,2,1,0:T(8,128)(2,1)S(1)}, u32[]{:S(2)}, u32[]{:S(2)}) collective-permute-start(bf16[1,1,32,64]{3,2,1,0:T(8,128)(2,1)S(1)} %fusion.23), channel_id=1, source_target_pairs={{0,4},{1,5},{2,6},{3,7},{8,12},{9,13},{10,14},{11,15},{16,20},{17,... | collective-permute-start | bytes 12296 | tf_op jit(solution)/shard_map/ppermute | solution.py:16
  128.9 27.1 %copy-start.65 = (bf16[1,4,64,64]{3,2,1,0:T(8,128)(2,1)S(1)}, bf16[1,4,64,64]{3,2,1,0:T(8,128)(2,1)}, u32[]{:S(2)}) copy-start(bf16[1,4,64,64]{3,2,1,0:T(8,128)(2,1)} %get-tuple-element.154) | copy-start | bytes 98308
  129.8 46.4 %copy-start.82 = (bf16[1,4,64,64]{3,2,1,0:T(8,128)(2,1)S(1)}, bf16[1,4,64,64]{3,2,1,0:T(8,128)(2,1)}, u32[]{:S(2)}) copy-start(bf16[1,4,64,64]{3,2,1,0:T(8,128)(2,1)} %get-tuple-element.153) | copy-start | bytes 98308
  129.8 18.0 %collective-permute-start.14 = (bf16[1,4,32,64]{3,2,1,0:T(8,128)(2,1)}, bf16[1,4,32,64]{3,2,1,0:T(8,128)(2,1)S(1)}, u32[]{:S(2)}, u32[]{:S(2)}) collective-permute-start(bf16[1,4,32,64]{3,2,1,0:T(8,128)(2,1)} %bitcast.34), channel_id=1, source_target_pairs={{16,0},{24,8},{17,1},{25,9},{18,2},{26,10},{19,3},{27,11},{20,4},{... | collective-permute-start | bytes 49160 | tf_op jit(solution)/shard_map/ppermute | solution.py:16
  132.0 17.2 %collective-permute-start.15 = (bf16[1,4,32,64]{3,2,1,0:T(8,128)(2,1)}, bf16[1,4,32,64]{3,2,1,0:T(8,128)(2,1)S(1)}, u32[]{:S(2)}, u32[]{:S(2)}) collective-permute-start(bf16[1,4,32,64]{3,2,1,0:T(8,128)(2,1)} %bitcast.34), channel_id=1, source_target_pairs={{24,0},{25,1},{26,2},{27,3},{28,4},{29,5},{30,6},{31,7}} | collective-permute-start | bytes 49160 | tf_op jit(solution)/shard_map/ppermute | solution.py:16
  134.0 124.7 %collective-permute-start.4 = (bf16[2,8,32,64]{3,2,1,0:T(8,128)(2,1)}, bf16[2,8,32,64]{3,2,1,0:T(8,128)(2,1)}, u32[]{:S(2)}, u32[]{:S(2)}) collective-permute-start(bf16[2,8,32,64]{3,2,1,0:T(8,128)(2,1)} %convolution_convert_fusion), channel_id=1, source_target_pairs={{0,16},{8,24},{1,17},{9,25},{2,18},{10,26},{3,19},{11,27},{4,20},{... | collective-permute-start | bytes 196616 | tf_op jit(solution)/shard_map/ppermute | solution.py:16
  138.8 122.1 %collective-permute-start.5 = (bf16[2,8,32,64]{3,2,1,0:T(8,128)(2,1)}, bf16[2,8,32,64]{3,2,1,0:T(8,128)(2,1)}, u32[]{:S(2)}, u32[]{:S(2)}) collective-permute-start(bf16[2,8,32,64]{3,2,1,0:T(8,128)(2,1)} %convolution_convert_fusion), channel_id=1, source_target_pairs={{0,8},{8,16},{16,24},{1,9},{9,17},{17,25},{2,10},{10,18},{18,26},{... | collective-permute-start | bytes 196616 | tf_op jit(solution)/shard_map/ppermute | solution.py:16
  144.7 127.9 %collective-permute-start.6 = (bf16[2,8,32,64]{3,2,1,0:T(8,128)(2,1)}, bf16[2,8,32,64]{3,2,1,0:T(8,128)(2,1)}, u32[]{:S(2)}, u32[]{:S(2)}) collective-permute-start(bf16[2,8,32,64]{3,2,1,0:T(8,128)(2,1)} %convolution_convert_fusion), channel_id=1, source_target_pairs={{8,0},{16,8},{24,16},{9,1},{17,9},{25,17},{10,2},{18,10},{26,18},{... | collective-permute-start | bytes 196616 | tf_op jit(solution)/shard_map/ppermute | solution.py:16
  147.8 149.0 %collective-permute-start.7 = (bf16[2,8,32,64]{3,2,1,0:T(8,128)(2,1)}, bf16[2,8,32,64]{3,2,1,0:T(8,128)(2,1)}, u32[]{:S(2)}, u32[]{:S(2)}) collective-permute-start(bf16[2,8,32,64]{3,2,1,0:T(8,128)(2,1)} %convolution_convert_fusion), channel_id=1, source_target_pairs={{16,0},{24,8},{17,1},{25,9},{18,2},{26,10},{19,3},{27,11},{20,4},{... | collective-permute-start | bytes 196616 | tf_op jit(solution)/shard_map/ppermute | solution.py:16
  149.1 5.1 %collective-permute-start.19 = (bf16[1,2,32,64]{3,2,1,0:T(8,128)(2,1)S(1)}, bf16[1,2,32,64]{3,2,1,0:T(8,128)(2,1)S(1)}, u32[]{:S(2)}, u32[]{:S(2)}) collective-permute-start(bf16[1,2,32,64]{3,2,1,0:T(8,128)(2,1)S(1)} %bitcast.607), channel_id=1, source_target_pairs={{16,0},{24,8},{17,1},{25,9},{18,2},{26,10},{19,3},{27,11},{20,4},{... | collective-permute-start | bytes 24584 | tf_op jit(solution)/shard_map/ppermute | solution.py:16
  150.5 51.9 %copy-start.52 = (bf16[7,4,32,64]{3,2,1,0:T(8,128)(2,1)}, bf16[7,4,32,64]{3,2,1,0:T(8,128)(2,1)S(1)}, u32[]{:S(2)}) copy-start(bf16[7,4,32,64]{3,2,1,0:T(8,128)(2,1)S(1)} %constant_dynamic-update-slice_fusion.18) | copy-start | bytes 344068
  154.3 3.1 collective-permute-start.18
  157.3 8.7 %collective-permute-start.28 = (bf16[1,2,1,32,64]{4,3,2,1,0:T(8,128)(2,1)S(1)}, bf16[1,2,1,32,64]{4,3,2,1,0:T(8,128)(2,1)S(1)}, u32[]{:S(2)}, u32[]{:S(2)}) collective-permute-start(bf16[1,2,1,32,64]{4,3,2,1,0:T(8,128)(2,1)S(1)} %get-tuple-element.333), channel_id=1, source_target_pairs={{1,0},{2,1},{3,2},{4,3},{5,4},{6,5},{7,6},{9,8},{10,9},{11,10},{12... | collective-permute-start | bytes 24584 | tf_op jit(solution)/shard_map/ppermute | solution.py:16
  168.3 4.9 %collective-permute-start.35 = (bf16[1,2,1,32,64]{4,3,2,1,0:T(8,128)(2,1)S(1)}, bf16[1,2,1,32,64]{4,3,2,1,0:T(8,128)(2,1)S(1)}, u32[]{:S(2)}, u32[]{:S(2)}) collective-permute-start(bf16[1,2,1,32,64]{4,3,2,1,0:T(8,128)(2,1)S(1)} %get-tuple-element.331), channel_id=1, source_target_pairs={{2,0},{3,1},{4,2},{5,3},{6,4},{7,5},{10,8},{11,9},{12,10},{13,11},... | collective-permute-start | bytes 24584 | tf_op jit(solution)/shard_map/ppermute | solution.py:16
  173.1 5.0 %collective-permute-start.27 = (bf16[7,1,32,64]{3,2,1,0:T(8,128)(2,1)}, bf16[7,1,32,64]{3,2,1,0:T(8,128)(2,1)S(1)}, u32[]{:S(2)}, u32[]{:S(2)}) collective-permute-start(bf16[7,1,32,64]{3,2,1,0:T(8,128)(2,1)} %constant_dynamic-update-slice_fusion.30), channel_id=1, source_target_pairs={{0,3},{1,4},{2,5},{3,6},{4,7},{8,11},{9,12},{10,13},{11,14},{12,15... | collective-permute-start | bytes 86024 | tf_op jit(solution)/shard_map/ppermute | solution.py:16
  178.2 5.3 %collective-permute-start.22 = (bf16[7,1,32,64]{3,2,1,0:T(8,128)(2,1)}, bf16[7,1,32,64]{3,2,1,0:T(8,128)(2,1)S(1)}, u32[]{:S(2)}, u32[]{:S(2)}) collective-permute-start(bf16[7,1,32,64]{3,2,1,0:T(8,128)(2,1)} %constant_dynamic-update-slice_fusion.30), channel_id=1, source_target_pairs={{0,2},{1,3},{2,4},{3,5},{4,6},{5,7},{8,10},{9,11},{10,12},{11,13},... | collective-permute-start | bytes 86024 | tf_op jit(solution)/shard_map/ppermute | solution.py:16
  183.4 5.8 %collective-permute-start.23 = (bf16[7,1,32,64]{3,2,1,0:T(8,128)(2,1)}, bf16[7,1,32,64]{3,2,1,0:T(8,128)(2,1)S(1)}, u32[]{:S(2)}, u32[]{:S(2)}) collective-permute-start(bf16[7,1,32,64]{3,2,1,0:T(8,128)(2,1)} %constant_dynamic-update-slice_fusion.30), channel_id=1, source_target_pairs={{0,1},{1,2},{2,3},{3,4},{4,5},{5,6},{6,7},{8,9},{9,10},{10,11},{11... | collective-permute-start | bytes 86024 | tf_op jit(solution)/shard_map/ppermute | solution.py:16
  189.2 6.2 %collective-permute-start.24 = (bf16[7,1,32,64]{3,2,1,0:T(8,128)(2,1)}, bf16[7,1,32,64]{3,2,1,0:T(8,128)(2,1)S(1)}, u32[]{:S(2)}, u32[]{:S(2)}) collective-permute-start(bf16[7,1,32,64]{3,2,1,0:T(8,128)(2,1)} %constant_dynamic-update-slice_fusion.30), channel_id=1, source_target_pairs={{1,0},{2,1},{3,2},{4,3},{5,4},{6,5},{7,6},{9,8},{10,9},{11,10},{12... | collective-permute-start | bytes 86024 | tf_op jit(solution)/shard_map/ppermute | solution.py:16
  195.4 5.6 %collective-permute-start.25 = (bf16[7,1,32,64]{3,2,1,0:T(8,128)(2,1)}, bf16[7,1,32,64]{3,2,1,0:T(8,128)(2,1)S(1)}, u32[]{:S(2)}, u32[]{:S(2)}) collective-permute-start(bf16[7,1,32,64]{3,2,1,0:T(8,128)(2,1)} %constant_dynamic-update-slice_fusion.30), channel_id=1, source_target_pairs={{2,0},{3,1},{4,2},{5,3},{6,4},{7,5},{10,8},{11,9},{12,10},{13,11},... | collective-permute-start | bytes 86024 | tf_op jit(solution)/shard_map/ppermute | solution.py:16
  201.1 6.7 %collective-permute-start.26 = (bf16[7,1,32,64]{3,2,1,0:T(8,128)(2,1)}, bf16[7,1,32,64]{3,2,1,0:T(8,128)(2,1)}, u32[]{:S(2)}, u32[]{:S(2)}) collective-permute-start(bf16[7,1,32,64]{3,2,1,0:T(8,128)(2,1)} %constant_dynamic-update-slice_fusion.30), channel_id=1, source_target_pairs={{3,0},{4,1},{5,2},{6,3},{7,4},{11,8},{12,9},{13,10},{14,11},{15,12... | collective-permute-start | bytes 86024 | tf_op jit(solution)/shard_map/ppermute | solution.py:16
  207.8 13.1 %collective-permute-start.34 = (bf16[7,1,32,64]{3,2,1,0:T(8,128)(2,1)}, bf16[7,1,32,64]{3,2,1,0:T(8,128)(2,1)}, u32[]{:S(2)}, u32[]{:S(2)}) collective-permute-start(bf16[7,1,32,64]{3,2,1,0:T(8,128)(2,1)} %constant_dynamic-update-slice_fusion.35), channel_id=1, source_target_pairs={{0,6},{1,7},{8,14},{9,15},{16,22},{17,23},{24,30},{25,31}} | collective-permute-start | bytes 86024 | tf_op jit(solution)/shard_map/ppermute | solution.py:16
  220.8 2.8 collective-permute-start.29
  223.5 23.2 %copy-start.72 = (bf16[1,1,32,64]{3,2,1,0:T(8,128)(2,1)}, bf16[1,1,32,64]{3,2,1,0:T(8,128)(2,1)S(1)}, u32[]{:S(2)}) copy-start(bf16[1,1,32,64]{3,2,1,0:T(8,128)(2,1)S(1)} %get-tuple-element.230) | copy-start | bytes 12292
  223.5 23.2 %copy-start.73 = (bf16[1,1,32,64]{3,2,1,0:T(8,128)(2,1)}, bf16[1,1,32,64]{3,2,1,0:T(8,128)(2,1)S(1)}, u32[]{:S(2)}) copy-start(bf16[1,1,32,64]{3,2,1,0:T(8,128)(2,1)S(1)} %get-tuple-element.231) | copy-start | bytes 12292
  223.5 23.2 %copy-start.74 = (bf16[1,1,32,64]{3,2,1,0:T(8,128)(2,1)}, bf16[1,1,32,64]{3,2,1,0:T(8,128)(2,1)S(1)}, u32[]{:S(2)}) copy-start(bf16[1,1,32,64]{3,2,1,0:T(8,128)(2,1)S(1)} %get-tuple-element.232) | copy-start | bytes 12292
  223.5 23.3 %copy-start.75 = (bf16[1,1,32,64]{3,2,1,0:T(8,128)(2,1)}, bf16[1,1,32,64]{3,2,1,0:T(8,128)(2,1)S(1)}, u32[]{:S(2)}) copy-start(bf16[1,1,32,64]{3,2,1,0:T(8,128)(2,1)S(1)} %get-tuple-element.233) | copy-start | bytes 12292
  223.7 3.3 collective-permute-start.30
  226.0 20.8 %copy-start.76 = (bf16[1,1,32,64]{3,2,1,0:T(8,128)(2,1)}, bf16[1,1,32,64]{3,2,1,0:T(8,128)(2,1)S(1)}, u32[]{:S(2)}) copy-start(bf16[1,1,32,64]{3,2,1,0:T(8,128)(2,1)S(1)} %get-tuple-element.221) | copy-start | bytes 12292
  227.0 6.8 %collective-permute-start.31 = (bf16[7,1,32,64]{3,2,1,0:T(8,128)(2,1)}, bf16[7,1,32,64]{3,2,1,0:T(8,128)(2,1)S(1)}, u32[]{:S(2)}, u32[]{:S(2)}) collective-permute-start(bf16[7,1,32,64]{3,2,1,0:T(8,128)(2,1)} %constant_dynamic-update-slice_fusion.35), channel_id=1, source_target_pairs={{2,0},{3,1},{4,2},{5,3},{6,4},{7,5},{10,8},{11,9},{12,10},{13,11},... | collective-permute-start | bytes 86024 | tf_op jit(solution)/shard_map/ppermute | solution.py:16
  228.9 17.9 %copy-start.80 = (bf16[1,1,32,64]{3,2,1,0:T(8,128)(2,1)}, bf16[1,1,32,64]{3,2,1,0:T(8,128)(2,1)S(1)}, u32[]{:S(2)}) copy-start(bf16[1,1,32,64]{3,2,1,0:T(8,128)(2,1)S(1)} %get-tuple-element.217) | copy-start | bytes 12292
  233.7 6.0 %collective-permute-start.32 = (bf16[7,1,32,64]{3,2,1,0:T(8,128)(2,1)}, bf16[7,1,32,64]{3,2,1,0:T(8,128)(2,1)S(1)}, u32[]{:S(2)}, u32[]{:S(2)}) collective-permute-start(bf16[7,1,32,64]{3,2,1,0:T(8,128)(2,1)} %constant_dynamic-update-slice_fusion.35), channel_id=1, source_target_pairs={{4,0},{5,1},{6,2},{7,3},{12,8},{13,9},{14,10},{15,11},{20,16},{21,... | collective-permute-start | bytes 86024 | tf_op jit(solution)/shard_map/ppermute | solution.py:16
  235.6 11.2 %copy-start.81 = (bf16[1,1,32,64]{3,2,1,0:T(8,128)(2,1)}, bf16[1,1,32,64]{3,2,1,0:T(8,128)(2,1)S(1)}, u32[]{:S(2)}) copy-start(bf16[1,1,32,64]{3,2,1,0:T(8,128)(2,1)S(1)} %get-tuple-element.213) | copy-start | bytes 12292
  239.8 7.0 %collective-permute-start.33 = (bf16[7,1,32,64]{3,2,1,0:T(8,128)(2,1)}, bf16[7,1,32,64]{3,2,1,0:T(8,128)(2,1)}, u32[]{:S(2)}, u32[]{:S(2)}) collective-permute-start(bf16[7,1,32,64]{3,2,1,0:T(8,128)(2,1)} %constant_dynamic-update-slice_fusion.35), channel_id=1, source_target_pairs={{6,0},{7,1},{14,8},{15,9},{22,16},{23,17},{30,24},{31,25}} | collective-permute-start | bytes 86024 | tf_op jit(solution)/shard_map/ppermute | solution.py:16
  246.8 23.7 %collective-permute-start = (bf16[1,8,32,128]{3,2,1,0:T(8,128)(2,1)}, bf16[1,8,32,128]{3,2,1,0:T(8,128)(2,1)S(1)}, u32[]{:S(2)}, u32[]{:S(2)}) collective-permute-start(bf16[1,8,32,128]{3,2,1,0:T(8,128)(2,1)} %get-tuple-element.161), channel_id=1, source_target_pairs={{0,8},{8,16},{16,24},{1,9},{9,17},{17,25},{2,10},{10,18},{18,26},{... | collective-permute-start | bytes 196616 | tf_op jit(solution)/shard_map/ppermute | solution.py:26
  257.1 15.5 %copy-start.134 = (bf16[7,1,32,64]{3,2,1,0:T(8,128)(2,1)S(1)}, bf16[7,1,32,64]{3,2,1,0:T(8,128)(2,1)}, u32[]{:S(2)}) copy-start(bf16[7,1,32,64]{3,2,1,0:T(8,128)(2,1)} %constant_dynamic-update-slice_fusion.40) | copy-start | bytes 86020
  258.7 44.1 %collective-permute-start.1 = (bf16[1,8,32,128]{3,2,1,0:T(8,128)(2,1)}, bf16[1,8,32,128]{3,2,1,0:T(8,128)(2,1)}, u32[]{:S(2)}, u32[]{:S(2)}) collective-permute-start(bf16[1,8,32,128]{3,2,1,0:T(8,128)(2,1)} %get-tuple-element.160), channel_id=1, source_target_pairs={{8,0},{16,8},{24,16},{9,1},{17,9},{25,17},{10,2},{18,10},{26,18},{... | collective-permute-start | bytes 196616 | tf_op jit(solution)/shard_map/ppermute | solution.py:27
  260.9 76.6 %collective-permute-start.17 = (bf16[7,4,32,64]{3,2,1,0:T(8,128)(2,1)}, bf16[7,4,32,64]{3,2,1,0:T(8,128)(2,1)}, u32[]{:S(2)}, u32[]{:S(2)}) collective-permute-start(bf16[7,4,32,64]{3,2,1,0:T(8,128)(2,1)} %copy-done.52), channel_id=1, source_target_pairs={{1,0},{2,1},{3,2},{4,3},{5,4},{6,5},{7,6},{9,8},{10,9},{11,10},{12... | collective-permute-start | bytes 344072 | tf_op jit(solution)/shard_map/ppermute | solution.py:16
  270.6 18.9 %copy-start.66 = (bf16[1,8,32,128]{3,2,1,0:T(8,128)(2,1)}, bf16[1,8,32,128]{3,2,1,0:T(8,128)(2,1)S(1)}, u32[]{:S(2)}) copy-start(bf16[1,8,32,128]{3,2,1,0:T(8,128)(2,1)S(1)} %collective-permute-done) | copy-start | bytes 196612
  270.6 68.0 %collective-permute-start.16 = (bf16[7,4,32,64]{3,2,1,0:T(8,128)(2,1)}, bf16[7,4,32,64]{3,2,1,0:T(8,128)(2,1)}, u32[]{:S(2)}, u32[]{:S(2)}) collective-permute-start(bf16[7,4,32,64]{3,2,1,0:T(8,128)(2,1)} %copy-done.52), channel_id=1, source_target_pairs={{0,1},{1,2},{2,3},{3,4},{4,5},{5,6},{6,7},{8,9},{9,10},{10,11},{11... | collective-permute-start | bytes 344072 | tf_op jit(solution)/shard_map/ppermute | solution.py:16
  272.6 4.5 %collective-permute-start.36 = (bf16[7,1,32,64]{3,2,1,0:T(8,128)(2,1)S(1)}, bf16[7,1,32,64]{3,2,1,0:T(8,128)(2,1)S(1)}, u32[]{:S(2)}, u32[]{:S(2)}) collective-permute-start(bf16[7,1,32,64]{3,2,1,0:T(8,128)(2,1)S(1)} %copy-done.134), channel_id=1, source_target_pairs={{0,4},{1,5},{2,6},{3,7},{8,12},{9,13},{10,14},{11,15},{16,20},{17,... | collective-permute-start | bytes 86024 | tf_op jit(solution)/shard_map/ppermute | solution.py:16
  276.7 11.9 %copy-start.42 = (bf16[10,8,32,64]{3,2,1,0:T(8,128)(2,1)}, bf16[10,8,32,64]{3,2,1,0:T(8,128)(2,1)S(1)}, u32[]{:S(2)}) copy-start(bf16[10,8,32,64]{3,2,1,0:T(8,128)(2,1)S(1)} %constant_dynamic-update-slice_fusion.14) | copy-start | bytes 983044
  277.0 6.5 %collective-permute-start.37 = (bf16[7,1,32,64]{3,2,1,0:T(8,128)(2,1)S(1)}, bf16[7,1,32,64]{3,2,1,0:T(8,128)(2,1)S(1)}, u32[]{:S(2)}, u32[]{:S(2)}) collective-permute-start(bf16[7,1,32,64]{3,2,1,0:T(8,128)(2,1)S(1)} %copy-done.134), channel_id=1, source_target_pairs={{4,0},{5,1},{6,2},{7,3},{12,8},{13,9},{14,10},{15,11},{20,16},{21,... | collective-permute-start | bytes 86024 | tf_op jit(solution)/shard_map/ppermute | solution.py:16
  283.5 26.4 %collective-permute-start.20 = (bf16[7,2,32,64]{3,2,1,0:T(8,128)(2,1)}, bf16[7,2,32,64]{3,2,1,0:T(8,128)(2,1)}, u32[]{:S(2)}, u32[]{:S(2)}) collective-permute-start(bf16[7,2,32,64]{3,2,1,0:T(8,128)(2,1)} %constant_dynamic-update-slice_fusion.25), channel_id=1, source_target_pairs={{0,1},{1,2},{2,3},{3,4},{4,5},{5,6},{6,7},{8,9},{9,10},{10,11},{11... | collective-permute-start | bytes 172040 | tf_op jit(solution)/shard_map/ppermute | solution.py:16
  296.8 12.7 %copy-start.62 = (bf16[1,4,64,64]{3,2,1,0:T(8,128)(2,1)S(1)}, bf16[1,4,64,64]{3,2,1,0:T(8,128)(2,1)}, u32[]{:S(2)}) copy-start(bf16[1,4,64,64]{3,2,1,0:T(8,128)(2,1)} %get-tuple-element.148) | copy-start | bytes 98308
  296.8 2.3 collective-permute-start.39
  299.0 10.6 %copy-start.33 = (bf16[27,64,64]{2,1,0:T(8,128)(2,1)S(1)}, bf16[27,64,64]{2,1,0:T(8,128)(2,1)}, u32[]{:S(2)}) copy-start(bf16[27,64,64]{2,1,0:T(8,128)(2,1)} %broadcast_select_fusion.19) | copy-start | bytes 663556
  299.1 15.7 %collective-permute-start.21 = (bf16[7,2,32,64]{3,2,1,0:T(8,128)(2,1)}, bf16[7,2,32,64]{3,2,1,0:T(8,128)(2,1)S(1)}, u32[]{:S(2)}, u32[]{:S(2)}) collective-permute-start(bf16[7,2,32,64]{3,2,1,0:T(8,128)(2,1)} %constant_dynamic-update-slice_fusion.25), channel_id=1, source_target_pairs={{1,0},{2,1},{3,2},{4,3},{5,4},{6,5},{7,6},{9,8},{10,9},{11,10},{12... | collective-permute-start | bytes 172040 | tf_op jit(solution)/shard_map/ppermute | solution.py:16
  302.8 4.7 %collective-permute-start.40 = (bf16[1,1,32,64]{3,2,1,0:T(8,128)(2,1)S(1)}, bf16[1,1,32,64]{3,2,1,0:T(8,128)(2,1)S(1)}, u32[]{:S(2)}, u32[]{:S(2)}) collective-permute-start(bf16[1,1,32,64]{3,2,1,0:T(8,128)(2,1)S(1)} %fusion.25), channel_id=1, source_target_pairs={{0,1},{1,2},{2,3},{3,4},{4,5},{5,6},{6,7},{8,9},{9,10},{10,11},{11... | collective-permute-start | bytes 12296 | tf_op jit(solution)/shard_map/ppermute | solution.py:16
  307.5 34.8 %collective-permute-start.9 = (bf16[8,8,32,64]{3,2,1,0:T(8,128)(2,1)S(1)}, bf16[8,8,32,64]{3,2,1,0:T(8,128)(2,1)}, u32[]{:S(2)}, u32[]{:S(2)}) collective-permute-start(bf16[8,8,32,64]{3,2,1,0:T(8,128)(2,1)S(1)} %slice.1838), channel_id=1, source_target_pairs={{1,0},{2,1},{3,2},{4,3},{5,4},{6,5},{7,6},{9,8},{10,9},{11,10},{12... | collective-permute-start | bytes 786440 | tf_op jit(solution)/shard_map/ppermute | solution.py:16
  309.8 32.4 %collective-permute-start.8 = (bf16[8,8,32,64]{3,2,1,0:T(8,128)(2,1)S(1)}, bf16[8,8,32,64]{3,2,1,0:T(8,128)(2,1)}, u32[]{:S(2)}, u32[]{:S(2)}) collective-permute-start(bf16[8,8,32,64]{3,2,1,0:T(8,128)(2,1)S(1)} %slice.1838), channel_id=1, source_target_pairs={{0,1},{1,2},{2,3},{3,4},{4,5},{5,6},{6,7},{8,9},{9,10},{10,11},{11... | collective-permute-start | bytes 786440 | tf_op jit(solution)/shard_map/ppermute | solution.py:16
  314.8 6.2 %collective-permute-start.41 = (bf16[1,1,32,64]{3,2,1,0:T(8,128)(2,1)S(1)}, bf16[1,1,32,64]{3,2,1,0:T(8,128)(2,1)S(1)}, u32[]{:S(2)}, u32[]{:S(2)}) collective-permute-start(bf16[1,1,32,64]{3,2,1,0:T(8,128)(2,1)S(1)} %fusion.26), channel_id=1, source_target_pairs={{0,16},{8,24},{1,17},{9,25},{2,18},{10,26},{3,19},{11,27},{4,20},{... | collective-permute-start | bytes 12296 | tf_op jit(solution)/shard_map/ppermute | solution.py:16
  320.6 11.9 %copy-start.67 = (bf16[1,8,32,128]{3,2,1,0:T(8,128)(2,1)S(1)}, bf16[1,8,32,128]{3,2,1,0:T(8,128)(2,1)}, u32[]{:S(2)}) copy-start(bf16[1,8,32,128]{3,2,1,0:T(8,128)(2,1)} %copy-done.66) | copy-start | bytes 196612
  321.2 4.8 %collective-permute-start.42 = (bf16[1,2,32,64]{3,2,1,0:T(8,128)(2,1)S(1)}, bf16[1,2,32,64]{3,2,1,0:T(8,128)(2,1)S(1)}, u32[]{:S(2)}, u32[]{:S(2)}) collective-permute-start(bf16[1,2,32,64]{3,2,1,0:T(8,128)(2,1)S(1)} %fusion.90), channel_id=1, source_target_pairs={{0,8},{8,16},{16,24},{1,9},{9,17},{17,25},{2,10},{10,18},{18,26},{... | collective-permute-start | bytes 24584 | tf_op jit(solution)/shard_map/ppermute | solution.py:16
  326.0 4.5 %collective-permute-start.2 = (bf16[4,1,32,128]{3,2,1,0:T(8,128)(2,1)S(1)}, bf16[4,1,32,128]{3,2,1,0:T(8,128)(2,1)S(1)}, u32[]{:S(2)}, u32[]{:S(2)}) collective-permute-start(bf16[4,1,32,128]{3,2,1,0:T(8,128)(2,1)S(1)} %get-tuple-element.159), channel_id=1, source_target_pairs={{0,1},{1,2},{2,3},{3,4},{4,5},{5,6},{6,7},{8,9},{9,10},{10,11},{11... | collective-permute-start | bytes 98312 | tf_op jit(solution)/shard_map/ppermute | solution.py:26
  330.6 5.8 %collective-permute-start.3 = (bf16[4,1,32,128]{3,2,1,0:T(8,128)(2,1)S(1)}, bf16[4,1,32,128]{3,2,1,0:T(8,128)(2,1)S(1)}, u32[]{:S(2)}, u32[]{:S(2)}) collective-permute-start(bf16[4,1,32,128]{3,2,1,0:T(8,128)(2,1)S(1)} %get-tuple-element.158), channel_id=1, source_target_pairs={{1,0},{2,1},{3,2},{4,3},{5,4},{6,5},{7,6},{9,8},{10,9},{11,10},{12... | collective-permute-start | bytes 98312 | tf_op jit(solution)/shard_map/ppermute | solution.py:27
  (114 other events, 350.7 us)
where the time goes:
time: 355 us; the launch traced here: 351 us
  starting transfers between devices  120 us (34%)
  local copies, waits for them, and re-layouts  118 us (33%)
  waiting for transfers between devices  42.4 us (12%)
  matrix products  35.1 us (10%)
  other arithmetic  33.4 us (9%)
    ppermute x39, starting transfers between devices, shifted(): return lax.ppermute(block, axis, route)  109 us
    gather x32, local copies, waits for them, and re-layouts, far_terms(): jnp.take(coupling_level, ids_level[2 * type_row + type_col], axis=0)  56.6 us
    ppermute x39, waiting for transfers between devices, shifted(): return lax.ppermute(block, axis, route)  37.7 us
    select_n x26, other arithmetic, far_terms(): jnp.take(coupling_level, ids_level[2 * type_row + type_col], axis=0)  24.3 us
    dot_general x31, matrix products, far_terms(): jnp.einsum('ijpk,kq->ijpq', stacked, chosen, preferred_element_type=jnp.f...  23.3 us
    unnamed x296, local copies, waits for them, and re-layouts  20.4 us
    concatenate x24, local copies, waits for them, and re-layouts, far_terms(): stacked = jnp.concatenate(pieces, axis=3)  17 us
    slice x21, local copies, waits for them, and re-layouts, far_terms(): lax.slice(widened, (start_row, start_col, 0, 0), (start_row + 2 * count_r...  10.8 us
  transfers between devices with their start and end apart: 43, of which 17 were waited for; matrix products, arithmetic and copies ran while one was open for 48% of the time, Pallas kernels for 0%

commit v1 on v0

v1 whole, which is shorter than its diff:
```python
import functools

import jax
import jax.numpy as jnp
from jax import lax
from jax.experimental import pallas as pl
from jax.experimental.pallas import tpu as pltpu
from jax.sharding import PartitionSpec as P

LEAF_ROWS = 8
LEAF_COLS = 16
LENGTH_SCALE = 1.5
MESH = pl.DeviceIdType.MESH
BF16 = jnp.bfloat16
F32 = jnp.float32
AROUND = [(du, dv) for du in (-1, 0, 1) for dv in (-1, 0, 1) if (du, dv) != (0, 0)]


def slot_offsets(type_row, type_col):
    offsets = []
    for off_row in range(-2 - type_row, 4 - type_row):
        for off_col in range(-2 - type_col, 4 - type_col):
            if max(abs(off_row), abs(off_col)) > 1:
                offsets.append((off_row, off_col))
    return offsets


SLOT_OF = {
    (e, f): {offset: s for s, offset in enumerate(slot_offsets(e, f))} for e in (0, 1) for f in (0, 1)
}


class Plan:
    def __init__(self, rows_dev, cols_dev, levels):
        self.rows_dev, self.cols_dev, self.levels = rows_dev, cols_dev, levels
        self.quads = rows_dev // 4
        self.pad = 2 if self.quads == 1 else 4
        self.window = 4 + 2 * self.pad
        self.grid = [(max(1, 2 * rows_dev >> l), max(1, 8 * cols_dev >> l)) for l in range(levels)]
        self.parents = [((r + 1) // 2, (c + 1) // 2) for r, c in self.grid]
        self.ne = [2 if r > 1 else 1 for r, _ in self.grid]
        self.offsets = [
            [(dr, dc) for dr, dc in AROUND if (pr > 1 or dr == 0) and (pc > 1 or dc == 0)]
            for pr, pc in self.parents
        ]
        self.top = max(l for l in range(levels) if self.offsets[l])
        self.far_levels = self.top + 1


def dot(a, b):
    return jnp.dot(a, b, preferred_element_type=F32)


def kernel(
    plan, probes, basis, up, down, coupling, ids, out,
    pbuf, s0, l1, l3, table, basis2, upv, downv, updup, downst, *rest,
):
    far_levels, top = plan.far_levels, plan.top
    weights, coup, rest = rest[:far_levels], rest[far_levels : 2 * far_levels], rest[2 * far_levels :]
    tops, rest = rest[: top - 2], rest[top - 2 :]
    local_sem, send_sem, precv, crecv, l1recv, l3recv = rest
    rows_dev, cols_dev, quads, pad = plan.rows_dev, plan.cols_dev, plan.quads, plan.pad
    g = lax.axis_index("gx")
    y = lax.axis_index("gy")
    quad, member = g // 4, g % 4
    quad_steps = (0,) if quads == 1 else (-1, 0, 1)

    def inside(row, col):
        return (row >= 0) & (row < rows_dev) & (col >= 0) & (col < cols_dev)

    near_partners = []
    for dq in quad_steps:
        for k in range(4):
            for dy in (-1, 0, 1):
                if (dq, k, dy) != (0, 0, 0):
                    near_partners.append((dq, k, dy))
    far_partners = [(kq, ky) for kq in range(quads) for ky in range(cols_dev) if (kq, ky) != (0, 0)]

    def near_device(dq, k, dy):
        return (quad + dq) * 4 + (member + k) % 4, y + dy

    def far_device(kq, ky):
        return (quad + kq) % quads * 4 + member, (y + ky) % cols_dev

    def met(row, col):
        return (abs(row // 4 - quad) <= 1) & (abs(col - y) <= 1)

    barrier = pltpu.get_barrier_semaphore()
    expected = jnp.int32(0)
    for partner in near_partners:
        row, col = near_device(*partner)
        valid = inside(row, col)

        @pl.when(valid)
        def _():
            pl.semaphore_signal(barrier, inc=1, device_id=(row, col), device_id_type=MESH)

        expected = expected + jnp.where(valid, 1, 0)
    for partner in far_partners:
        row, col = far_device(*partner)
        valid = jnp.logical_not(met(row, col))

        @pl.when(valid)
        def _():
            pl.semaphore_signal(barrier, inc=1, device_id=(row, col), device_id_type=MESH)

        expected = expected + jnp.where(valid, 1, 0)

    fetch = [
        pltpu.make_async_copy(probes, pbuf.at[1:3, 1:9], local_sem.at[0]),
        pltpu.make_async_copy(up.at[0:top], upv, local_sem.at[1]),
        pltpu.make_async_copy(down.at[0:top], downv, local_sem.at[2]),
    ]
    fetch_coup = [
        pltpu.make_async_copy(coupling.at[l], coup[l], local_sem.at[3 + l]) for l in range(far_levels)
    ]
    for copy in fetch + fetch_coup:
        copy.start()

    p_row_src = {0: slice(1, 3), 1: slice(2, 3), -1: slice(1, 2)}
    p_row_dst = {0: slice(1, 3), 1: slice(0, 1), -1: slice(3, 4)}
    p_col_src = {0: slice(1, 9), 1: slice(8, 9), -1: slice(1, 2)}
    p_col_dst = {0: slice(1, 9), 1: slice(0, 1), -1: slice(9, 10)}
    c_row_dst = {0: slice(1, 2), 1: slice(0, 1), -1: slice(2, 3)}
    c_col_src = {0: slice(1, 5), 1: slice(4, 5), -1: slice(1, 2)}
    c_col_dst = {0: slice(1, 5), 1: slice(0, 1), -1: slice(5, 6)}

    for du, dv in AROUND:

        @pl.when(jnp.logical_not(inside(g - du, y - dv)))
        def _():
            part = pbuf.at[p_row_dst[du], p_col_dst[dv]]
            part[...] = jnp.zeros(part.shape, BF16)
            part = s0.at[c_row_dst[du], c_col_dst[dv]]
            part[...] = jnp.zeros(part.shape, BF16)

    def clear(part):
        part[...] = jnp.zeros(part.shape, BF16)

    if quads == 1:
        clear(l1.at[0:pad])
        clear(l1.at[pad + 4 : 2 * pad + 4])
    else:

        @pl.when(quad == 0)
        def _():
            clear(l1.at[0:4])

        @pl.when(quad == quads - 1)
        def _():
            clear(l1.at[8:12])

    @pl.when(y == 0)
    def _():
        clear(l1.at[:, 0])

    @pl.when(y == cols_dev - 1)
    def _():
        clear(l1.at[:, 2])

    for level_top in tops:
        clear(level_top)

    basis_wide = basis[...]
    nothing = jnp.zeros((128, 64), BF16)
    basis2[0:128] = jnp.concatenate([basis_wide, nothing], axis=1)
    basis2[128:256] = jnp.concatenate([nothing, basis_wide], axis=1)

    fetch[1].wait()

    def make_updup(l):
        width = plan.ne[l] * 128
        wide = upv[l, 0 : 2 * plan.ne[l]].reshape(width, 64)
        updup[l, 0:width] = jnp.concatenate([wide, wide], axis=1)

    make_updup(0)
    fetch[0].wait()
    left_rows = jnp.concatenate(
        [
            jnp.concatenate([pbuf[1 + e, 1 + 2 * p], pbuf[1 + e, 2 + 2 * p]], axis=1)
            for e in (0, 1)
            for p in range(4)
        ],
        axis=0,
    )
    leaf = dot(left_rows, basis2[...]).astype(BF16)
    own = jnp.concatenate([leaf[0:128], leaf[128:256]], axis=1)
    s0[1, 1:5] = own.reshape(4, 32, 256)

    def halves(shape):
        return lax.broadcasted_iota(jnp.int32, shape, len(shape) - 1) // 64

    half32 = halves((32, 128))
    lifted = dot(own, updup[0, 0:256])
    own_row = pad + member
    for pc in (0, 1):
        first = lifted[64 * pc : 64 * pc + 32]
        second = lifted[64 * pc + 32 : 64 * pc + 64]
        l1[own_row, 1, pc] = jnp.where(half32 == 0, first, second).astype(BF16)

    pl.semaphore_wait(barrier, expected)

    sent = []

    def send(src, dst, recv, device, valid):
        copy = pltpu.make_async_remote_copy(
            src_ref=src, dst_ref=dst, send_sem=send_sem.at[len(sent)], recv_sem=recv,
            device_id=device, device_id_type=MESH,
        )
        sent.append((copy, valid))
        if valid is None:
            copy.start()
        else:
            pl.when(valid)(copy.start)

    def receive(dst, recv, valid):
        copy = pltpu.make_async_remote_copy(
            src_ref=dst, dst_ref=dst, send_sem=send_sem.at[0], recv_sem=recv,
            device_id=(g, y), device_id_type=MESH,
        )
        if valid is None:
            copy.wait_recv()
        else:
            pl.when(valid)(copy.wait_recv)

    ordered = sorted(near_partners, key=lambda t: (abs(t[2]), abs(t[0])))
    for dq, k, dy in ordered:
        device = near_device(dq, k, dy)
        row = pad - 4 * dq + member
        valid = None if (dq, dy) == (0, 0) else inside(*device)
        send(l1.at[own_row, 1], l1.at[row, 1 - dy], l1recv.at[row, 1 - dy], device, valid)
    for i, (du, dv) in sorted(enumerate(AROUND), key=lambda t: abs(t[1][1])):
        device = (g + du, y + dv)
        valid = inside(*device)
        send(s0.at[1:2, c_col_src[dv]], s0.at[c_row_dst[du], c_col_dst[dv]], crecv.at[i], device, valid)
        send(
            pbuf.at[p_row_src[du], p_col_src[dv]], pbuf.at[p_row_dst[du], p_col_dst[dv]],
            precv.at[i], device, valid,
        )

    for l in range(1, top):
        make_updup(l)

    def receive_l1(wanted):
        for dq, k, dy in ordered:
            if wanted(dq, dy):
                device = near_device(dq, k, dy)
                row = pad + 4 * dq + (member + k) % 4
                valid = None if (dq, dy) == (0, 0) else inside(*device)
                receive(l1.at[row, 1 + dy], l1recv.at[row, 1 + dy], valid)

    def level2(dq, side):
        parts = []
        for e in (0, 1):
            for pc in (0, 1):
                row = pad + 4 * dq + 2 * e
                parts.append(jnp.concatenate([l1[row, side, pc], l1[row + 1, side, pc]], axis=1))
        lift = dot(jnp.concatenate(parts, axis=0), updup[1, 0:256])
        both = [jnp.where(half32 == 0, lift[64 * e : 64 * e + 32], lift[64 * e + 32 : 64 * e + 64]) for e in (0, 1)]
        return jnp.concatenate(both, axis=1).astype(BF16)

    receive_l1(lambda dq, dy: dq == 0 and dy == 0)
    two = {(0, 0): level2(0, 1)}
    lift = dot(two[0, 0], updup[2, 0:256])
    l3[quad, y] = jnp.where(half32 == y % 2, lift, 0.0).astype(BF16)
    for kq, ky in far_partners:
        device = far_device(kq, ky)
        send(l3.at[quad, y], l3.at[quad, y], l3recv.at[quad, y], device, None)

    point_q = lax.broadcasted_iota(jnp.int32, (128, 128), 0)
    point_p = lax.broadcasted_iota(jnp.int32, (128, 128), 1)
    row_apart = (point_q // LEAF_COLS - point_p // LEAF_COLS).astype(F32)
    col_apart = (point_q % LEAF_COLS - point_p % LEAF_COLS).astype(F32)
    for i, (u, v) in enumerate([(u, v) for u in (-1, 0, 1) for v in (-1, 0, 1)]):
        dr = row_apart + float(u * LEAF_ROWS)
        dc = col_apart + float(v * LEAF_COLS)
        t = jnp.sqrt(3.0 * (dr * dr + dc * dc)) / LENGTH_SCALE
        table[128 * i : 128 * i + 128] = ((1.0 + t) * jnp.exp(-t)).astype(BF16)

    fetch[2].wait()
    for l in range(top):
        for e in range(plan.ne[l]):
            wide = jnp.concatenate([downv[l, 2 * e], downv[l, 2 * e + 1]], axis=1)
            for c in range(2 * plan.ne[l + 1]):
                downst[l, 64 * c : 64 * c + 64, 128 * e : 128 * e + 128] = wide

    empty = jnp.zeros((64, 64), BF16)
    for l in reversed(range(far_levels)):
        fetch_coup[l].wait()
        for i, (dr, dc) in enumerate(plan.offsets[l]):
            for se in range(plan.ne[l]):
                for sf in (0, 1):
                    for e in range(plan.ne[l]):
                        pair = []
                        for f in (0, 1):
                            slot = SLOT_OF[e, f].get((2 * dr + se - e, 2 * dc + sf - f))
                            pair.append(empty if slot is None else coup[l][ids[l, 2 * e + f, slot]])
                        c = 2 * se + sf
                        weights[l][i, 64 * c : 64 * c + 64, 128 * e : 128 * e + 128] = jnp.concatenate(pair, axis=1)

    receive_l1(lambda dq, dy: not (dq == 0 and dy == 0))
    pair_row = pad + 2 * (member // 2)
    far1 = jnp.zeros((64, 256), F32)
    for dr in (-1, 0, 1):
        row = pair_row + 2 * dr
        tiles = [
            jnp.concatenate([l1[row, side, pc], l1[row + 1, side, pc]], axis=1)
            for side, pc in ((0, 1), (1, 0), (1, 1), (2, 0))
        ]
        for dc in (-1, 0, 1):
            if (dr, dc) in plan.offsets[1]:
                lhs = jnp.concatenate([tiles[1 + dc], tiles[2 + dc]], axis=0)
                far1 = far1 + dot(lhs, weights[1][plan.offsets[1].index((dr, dc))])
    for dq in quad_steps:
        for dy in (-1, 0, 1):
            if (dq, dy) != (0, 0):
                two[dq, dy] = level2(dq, 1 + dy)
    far2 = jnp.zeros((32, 256), F32)
    for i, (dr, dc) in enumerate(plan.offsets[2]):
        far2 = far2 + dot(two[dr, dc], weights[2][i])

    for kq, ky in far_partners:
        row, col = (quad + kq) % quads, (y + ky) % cols_dev
        receive(l3.at[row, col], l3recv.at[row, col], None)
    for l in range(3, far_levels):
        pr_count, pc_count = plan.parents[l]
        level_top = tops[l - 3]
        if l == 3:
            for pr in range(pr_count):
                for pc in range(pc_count):
                    for e in range(plan.ne[3]):
                        level_top[1 + pr, 1 + pc, :, 128 * e : 128 * e + 128] = (
                            l3[2 * pr + e, 2 * pc] + l3[2 * pr + e, 2 * pc + 1]
                        )
        else:
            rows_below, cols_below = plan.grid[l]
            for r in range(rows_below):
                below = tops[l - 4][1 + r, 1 : 1 + cols_below].reshape(32 * cols_below, -1)
                lift = dot(below, updup[l - 1, 0 : below.shape[1]])
                for pc in range(pc_count):
                    first, second = lift[64 * pc : 64 * pc + 32], lift[64 * pc + 32 : 64 * pc + 64]
                    e = r % 2
                    level_top[1 + r // 2, 1 + pc, :, 128 * e : 128 * e + 128] = jnp.where(
                        half32 == 0, first, second
                    ).astype(BF16)

    def far_top(l):
        width = 128 * plan.ne[l]
        pr, pc = quad >> (l - 2), y >> (l - 2)
        total = jnp.zeros((32, width), F32)
        for i, (dr, dc) in enumerate(plan.offsets[l]):
            total = total + dot(tops[l - 3][1 + pr + dr, 1 + pc + dc], weights[l][i])
        return total

    local = None
    for l in reversed(range(3, far_levels)):
        total = far_top(l)
        if local is not None:
            total = total + dot(local, downst[l, 0 : local.shape[1], 0 : total.shape[1]])
        child = 2 * ((quad >> (l - 3)) % 2) + (y >> (l - 3)) % 2
        local = jnp.where(halves(total.shape) == child, total, 0.0).astype(BF16)
    total = far2 + dot(local, downst[2, 0 : local.shape[1], 0:256])
    lane = halves(total.shape)
    base = 2 * (g // 2 % 2)
    local = jnp.concatenate([jnp.where(lane == base + f, total, 0.0) for f in (0, 1)], axis=0).astype(BF16)
    total = far1 + dot(local, downst[1])
    base = 2 * (g % 2)
    local = jnp.concatenate(
        [jnp.where(lane == base + f, total[32 * pc : 32 * pc + 32], 0.0) for pc in (0, 1) for f in (0, 1)], axis=0
    ).astype(BF16)
    total = dot(local, downst[0])

    for i, (du, dv) in enumerate(AROUND):
        receive(s0.at[c_row_dst[du], c_col_dst[dv]], crecv.at[i], inside(g - du, y - dv))
    for i, (dr, dc) in enumerate(plan.offsets[0]):
        total = total + dot(s0[1 + dr, 1 + dc : 5 + dc].reshape(128, 256), weights[0][i])
    local = total.astype(BF16)
    local = jnp.concatenate([local[:, 0:128], local[:, 128:256]], axis=0)
    spread = lax.dot_general(local, basis2[...], (((1,), (1,)), ((), ())), preferred_element_type=F32)

    for i, (du, dv) in enumerate(AROUND):
        receive(pbuf.at[p_row_dst[du], p_col_dst[dv]], precv.at[i], inside(g - du, y - dv))
    for e in (0, 1):
        lhs = jnp.concatenate(
            [
                pbuf[1 + e + u, 1 + v : 9 + v].reshape(256, 128)
                for u in (-1, 0, 1)
                for v in (-1, 0, 1)
            ],
            axis=1,
        )
        near = dot(lhs, table[...])
        for b in range(8):
            p, f = b // 2, b % 2
            far = spread[128 * e + 32 * p : 128 * e + 32 * p + 32, 128 * f : 128 * f + 128]
            out[e, b] = (near[32 * b : 32 * b + 32] + far).astype(BF16)

    for copy, valid in sent:
        if valid is None:
            copy.wait_send()
        else:
            pl.when(valid)(copy.wait_send)


def shards(plan, probes, leaf_basis, up_transfer, down_transfer, coupling, far_ids):
    quads, cols_dev, far_levels, top = plan.quads, plan.cols_dev, plan.far_levels, plan.top
    dma = pltpu.SemaphoreType.DMA
    near_count = 3 * 4 * (1 if quads == 1 else 3) - 1
    send_count = near_count + 16 + quads * cols_dev - 1
    scratch = [
        pltpu.VMEM((4, 10, 32, 128), BF16),
        pltpu.VMEM((3, 6, 32, 256), BF16),
        pltpu.VMEM((plan.window, 3, 2, 32, 128), BF16),
        pltpu.VMEM((quads, cols_dev, 32, 128), BF16),
        pltpu.VMEM((9 * 128, 128), BF16),
        pltpu.VMEM((256, 128), BF16),
        pltpu.VMEM((top, 4, 64, 64), BF16),
        pltpu.VMEM((top, 4, 64, 64), BF16),
        pltpu.VMEM((top, 256, 128), BF16),
        pltpu.VMEM((top, 256, 256), BF16),
    ]
    for l in range(far_levels):
        scratch.append(pltpu.VMEM((len(plan.offsets[l]), 128 * plan.ne[l], 128 * plan.ne[l]), BF16))
    scratch += [pltpu.VMEM(coupling.shape[1:], BF16) for _ in range(far_levels)]
    for l in range(3, far_levels):
        pr, pc = plan.parents[l]
        scratch.append(pltpu.VMEM((pr + 2, pc + 2, 32, 128 * plan.ne[l]), BF16))
    scratch += [
        dma((3 + far_levels,)),
        dma((send_count,)),
        dma((8,)),
        dma((8,)),
        dma((plan.window, 3)),
        dma((quads, cols_dev)),
    ]
    anywhere = pl.BlockSpec(memory_space=pl.ANY)
    vmem = pl.BlockSpec(memory_space=pltpu.VMEM)
    return pl.pallas_call(
        functools.partial(kernel, plan),
        out_shape=jax.ShapeDtypeStruct(probes.shape, BF16),
        in_specs=[anywhere, vmem, anywhere, anywhere, anywhere, pl.BlockSpec(memory_space=pltpu.SMEM)],
        out_specs=vmem,
        scratch_shapes=scratch,
        compiler_params=pltpu.CompilerParams(
            collective_id=0, has_side_effects=True, vmem_limit_bytes=40 * 1024 * 1024
        ),
    )(probes, leaf_basis, up_transfer, down_transfer, coupling, far_ids)


def solution(mesh):
    in_specs = (P("gx", "gy", None, None), P(), P(), P(), P(), P())
    out_specs = P("gx", "gy", None, None)

    def run(probes, leaf_basis, up_transfer, down_transfer, coupling, far_ids):
        plan = Plan(mesh.shape["gx"], mesh.shape["gy"], coupling.shape[0])
        return jax.shard_map(
            functools.partial(shards, plan), mesh=mesh, in_specs=in_specs, out_specs=out_specs, check_vma=False
        )(probes, leaf_basis, up_transfer, down_transfer, coupling, far_ids)

    return run
```

time: 355 us -> 26.5 us (0.07); the launches traced: 351 us -> 26.2 us
  starting transfers between devices: 120 us -> 0 us
  local copies, waits for them, and re-layouts: 118 us -> 7.63 us
  waiting for transfers between devices: 42.4 us -> 0 us
  matrix products: 35.1 us -> 0 us
  other arithmetic: 33.4 us -> 0 us
  Pallas kernels: 0 us -> 18.5 us
    ppermute x43 -> x0, starting transfers between devices: 120 us -> none  [the longest x39 109 us: shifted(): return lax.ppermute(block, axis, route)]
    gather x32 -> x0, local copies, waits for them, and re-layouts: 56.6 us -> none  [far_terms(): jnp.take(coupling_level, ids_level[2 * type_row + type_col], axis=0)]
    ppermute x43 -> x0, waiting for transfers between devices: 42.4 us -> none  [the longest x39 37.7 us: shifted(): return lax.ppermute(block, axis, route)]
    dot_general x46 -> x0, matrix products: 35.1 us -> none  [the longest x31 23.3 us: far_terms(): jnp.einsum('ijpk,kq->ijpq', stacked, chosen, preferred_element_type=jnp.f...]
    select_n x30 -> x0, other arithmetic: 25.8 us -> none  [the longest x26 24.3 us: far_terms(): jnp.take(coupling_level, ids_level[2 * type_row + type_col], axis=0)]
    concatenate x31 -> x0, local copies, waits for them, and re-layouts: 21.2 us -> none  [the longest x24 17 us: far_terms(): stacked = jnp.concatenate(pieces, axis=3)]
    pallas_call x0 -> x1, Pallas kernels: none -> 18.5 us  [shards(): pl.pallas_call(functools.partial(kernel, plan), out_shape=jax.ShapeDtypeS...]
    slice x26 -> x0, local copies, waits for them, and re-layouts: 14.1 us -> none  [the longest x21 10.8 us: far_terms(): lax.slice(widened, (start_row, start_col, 0, 0), (start_row + 2 * count_r...]
  transfers between devices with their start and end apart: 43 -> 0, of which waited for: 17 -> 0; matrix products, arithmetic and copies ran while one was open for 48% -> 0% of each run, Pallas kernels for 0% -> 0%
where the time goes in v1:
time: 26.5 us; the launch traced here: 26.2 us
  Pallas kernels  18.5 us (70%)
  local copies, waits for them, and re-layouts  7.63 us (29%)
    pallas_call x1, Pallas kernels, shards(): pl.pallas_call(functools.partial(kernel, plan), out_shape=jax.ShapeDtypeS...  18.5 us
    unnamed x12, local copies, waits for them, and re-layouts  7.63 us

profile of v1, /device:TPU:1, one launch (start us, length us, event | category | flops | bytes accessed | tf_op | source)
XLA Modules:
  0.0 26.2 jit_solution(5681100273861482424)
XLA Ops:
  0.0 0.8 %copy.7.basis = bf16[128,64]{1,0:T(8,128)(2,1)S(1)} copy(bf16[128,64]{0,1:T(8,128)(2,1)} %param.7) | data formatting | bytes 32768 | tf_op args[1]
  0.8 0.0 copy-start
  0.8 2.5 %copy-done = bf16[8,40,64,64]{3,2,1,0:T(8,128)(2,1)S(1)} copy-done((bf16[8,40,64,64]{3,2,1,0:T(8,128)(2,1)S(1)}, bf16[8,40,64,64]{3,2,1,0:T(8,128)(2,1)}, u32[]{:S(2)}) %copy-start) | copy-done | bytes 2621464
  3.3 0.0 copy-start.1
  3.3 1.0 %copy-done.1 = bf16[7,4,64,64]{3,2,1,0:T(8,128)(2,1)S(1)} copy-done((bf16[7,4,64,64]{3,2,1,0:T(8,128)(2,1)S(1)}, bf16[7,4,64,64]{3,2,1,0:T(8,128)(2,1)}, u32[]{:S(2)}) %copy-start.1) | copy-done | bytes 229400
  4.3 0.0 copy-start.2
  4.3 1.0 %copy-done.2 = bf16[7,4,64,64]{3,2,1,0:T(8,128)(2,1)S(1)} copy-done((bf16[7,4,64,64]{3,2,1,0:T(8,128)(2,1)S(1)}, bf16[7,4,64,64]{3,2,1,0:T(8,128)(2,1)}, u32[]{:S(2)}) %copy-start.2) | copy-done | bytes 229400
  5.4 0.0 copy-start.3
  5.4 0.9 %copy-done.3 = bf16[2,8,32,128]{3,2,1,0:T(8,128)(2,1)S(1)} copy-done((bf16[2,8,32,128]{3,2,1,0:T(8,128)(2,1)S(1)}, bf16[2,8,32,128]{3,2,1,0:T(8,128)(2,1)}, u32[]{:S(2)}) %copy-start.3) | copy-done | bytes 131096
  6.3 0.0 copy-start.4
  6.3 0.7 %copy-done.4 = s32[8,4,27]{2,1,0:T(4,128)S(1)} copy-done((s32[8,4,27]{2,1,0:T(4,128)S(1)}, s32[8,4,27]{2,1,0:T(4,128)}, u32[]{:S(2)}) %copy-start.4) | copy-done | bytes 3480
  7.0 18.5 %shard_map.64 = bf16[2,8,32,128]{3,2,1,0:T(8,128)(2,1)S(1)} custom-call(bf16[2,8,32,128]{3,2,1,0:T(8,128)(2,1)S(1)} %copy-done.3, bf16[128,64]{1,0:T(8,128)(2,1)S(1)} %copy.7.basis, bf16[7,4,64,64]{3,2,1,0:T(8,128)(2,1)S(1)} %copy-done.1, bf16[7,4,64,64]{3,2,1,0:T(8,128)(2,1)S(1)} %copy-done.2, bf16[8,40,64,64]{3,2,1,0:T(8,128)(2,1)S(1)} %copy-done, ...), custom_call_target="tpu_custom_call" | custom-call | tf_op jit(solution)/shard_map/pallas_call | solution.py:438
  25.5 0.7 %copy.9 = bf16[2,8,32,128]{3,2,1,0:T(8,128)(2,1)} copy(bf16[2,8,32,128]{3,2,1,0:T(8,128)(2,1)S(1)} %shard_map.64) | data formatting | bytes 262144
Async XLA Ops:
  0.8 2.5 %copy-start = (bf16[8,40,64,64]{3,2,1,0:T(8,128)(2,1)S(1)}, bf16[8,40,64,64]{3,2,1,0:T(8,128)(2,1)}, u32[]{:S(2)}) copy-start(bf16[8,40,64,64]{3,2,1,0:T(8,128)(2,1)} %coupling.1) | copy-start | bytes 7864324
  3.3 1.0 %copy-start.1 = (bf16[7,4,64,64]{3,2,1,0:T(8,128)(2,1)S(1)}, bf16[7,4,64,64]{3,2,1,0:T(8,128)(2,1)}, u32[]{:S(2)}) copy-start(bf16[7,4,64,64]{3,2,1,0:T(8,128)(2,1)} %up.1) | copy-start | bytes 688132
  4.3 1.0 %copy-start.2 = (bf16[7,4,64,64]{3,2,1,0:T(8,128)(2,1)S(1)}, bf16[7,4,64,64]{3,2,1,0:T(8,128)(2,1)}, u32[]{:S(2)}) copy-start(bf16[7,4,64,64]{3,2,1,0:T(8,128)(2,1)} %down.1) | copy-start | bytes 688132
  5.4 0.9 %copy-start.3 = (bf16[2,8,32,128]{3,2,1,0:T(8,128)(2,1)S(1)}, bf16[2,8,32,128]{3,2,1,0:T(8,128)(2,1)}, u32[]{:S(2)}) copy-start(bf16[2,8,32,128]{3,2,1,0:T(8,128)(2,1)} %probes.1) | copy-start | bytes 393220
  6.3 0.7 %copy-start.4 = (s32[8,4,27]{2,1,0:T(4,128)S(1)}, s32[8,4,27]{2,1,0:T(4,128)}, u32[]{:S(2)}) copy-start(s32[8,4,27]{2,1,0:T(4,128)} %ids.1) | copy-start | bytes 10372

commit v2 on v1

--- a/solution.py
+++ b/solution.py
@@ -52,8 +52,8 @@
 
 
 def kernel(
-    plan, probes, basis, up, down, coupling, ids, out,
-    pbuf, s0, l1, l3, table, basis2, upv, downv, updup, downst, *rest,
+    plan, probes, basis, up, down, coupling, ids_hbm, out,
+    pbuf, s0, l1, l3, table, basisv, ids, basis2, upv, downv, updup, downst, *rest,
 ):
     far_levels, top = plan.far_levels, plan.top
     weights, coup, rest = rest[:far_levels], rest[far_levels : 2 * far_levels], rest[2 * far_levels :]
@@ -110,9 +110,11 @@
         pltpu.make_async_copy(probes, pbuf.at[1:3, 1:9], local_sem.at[0]),
         pltpu.make_async_copy(up.at[0:top], upv, local_sem.at[1]),
         pltpu.make_async_copy(down.at[0:top], downv, local_sem.at[2]),
+        pltpu.make_async_copy(basis, basisv, local_sem.at[3]),
+        pltpu.make_async_copy(ids_hbm, ids, local_sem.at[4]),
     ]
     fetch_coup = [
-        pltpu.make_async_copy(coupling.at[l], coup[l], local_sem.at[3 + l]) for l in range(far_levels)
+        pltpu.make_async_copy(coupling.at[l], coup[l], local_sem.at[5 + l]) for l in range(far_levels)
     ]
     for copy in fetch + fetch_coup:
         copy.start()
@@ -161,10 +163,10 @@
     for level_top in tops:
         clear(level_top)
 
-    basis_wide = basis[...]
-    nothing = jnp.zeros((128, 64), BF16)
-    basis2[0:128] = jnp.concatenate([basis_wide, nothing], axis=1)
-    basis2[128:256] = jnp.concatenate([nothing, basis_wide], axis=1)
+    basis2[...] = jnp.zeros((128, 256), BF16)
+    fetch[3].wait()
+    basis2[0:64, 0:128] = basisv[...]
+    basis2[64:128, 128:256] = basisv[...]
 
     fetch[1].wait()
 
@@ -183,7 +185,9 @@
         ],
         axis=0,
     )
-    leaf = dot(left_rows, basis2[...]).astype(BF16)
+    leaf = lax.dot_general(
+        left_rows, basis2[...], (((1,), (1,)), ((), ())), preferred_element_type=F32
+    ).astype(BF16)
     own = jnp.concatenate([leaf[0:128], leaf[128:256]], axis=1)
     s0[1, 1:5] = own.reshape(4, 32, 256)
 
@@ -285,6 +289,7 @@
                 downst[l, 64 * c : 64 * c + 64, 128 * e : 128 * e + 128] = wide
 
     empty = jnp.zeros((64, 64), BF16)
+    fetch[4].wait()
     for l in reversed(range(far_levels)):
         fetch_coup[l].wait()
         for i, (dr, dc) in enumerate(plan.offsets[l]):
@@ -376,7 +381,7 @@
         total = total + dot(s0[1 + dr, 1 + dc : 5 + dc].reshape(128, 256), weights[0][i])
     local = total.astype(BF16)
     local = jnp.concatenate([local[:, 0:128], local[:, 128:256]], axis=0)
-    spread = lax.dot_general(local, basis2[...], (((1,), (1,)), ((), ())), preferred_element_type=F32)
+    spread = dot(local, basis2[...])
 
     for i, (du, dv) in enumerate(AROUND):
         receive(pbuf.at[p_row_dst[du], p_col_dst[dv]], precv.at[i], inside(g - du, y - dv))
@@ -413,7 +418,9 @@
         pltpu.VMEM((plan.window, 3, 2, 32, 128), BF16),
         pltpu.VMEM((quads, cols_dev, 32, 128), BF16),
         pltpu.VMEM((9 * 128, 128), BF16),
-        pltpu.VMEM((256, 128), BF16),
+        pltpu.VMEM((64, 128), BF16),
+        pltpu.SMEM(far_ids.shape, jnp.int32),
+        pltpu.VMEM((128, 256), BF16),
         pltpu.VMEM((top, 4, 64, 64), BF16),
         pltpu.VMEM((top, 4, 64, 64), BF16),
         pltpu.VMEM((top, 256, 128), BF16),
@@ -426,25 +433,25 @@
         pr, pc = plan.parents[l]
         scratch.append(pltpu.VMEM((pr + 2, pc + 2, 32, 128 * plan.ne[l]), BF16))
     scratch += [
-        dma((3 + far_levels,)),
+        dma((5 + far_levels,)),
         dma((send_count,)),
         dma((8,)),
         dma((8,)),
         dma((plan.window, 3)),
         dma((quads, cols_dev)),
     ]
-    anywhere = pl.BlockSpec(memory_space=pl.ANY)
+    anywhere = pl.BlockSpec(memory_space=pltpu.HBM)
     vmem = pl.BlockSpec(memory_space=pltpu.VMEM)
     return pl.pallas_call(
         functools.partial(kernel, plan),
         out_shape=jax.ShapeDtypeStruct(probes.shape, BF16),
-        in_specs=[anywhere, vmem, anywhere, anywhere, anywhere, pl.BlockSpec(memory_space=pltpu.SMEM)],
+        in_specs=[anywhere] * 6,
         out_specs=vmem,
         scratch_shapes=scratch,
         compiler_params=pltpu.CompilerParams(
-            collective_id=0, has_side_effects=True, vmem_limit_bytes=40 * 1024 * 1024
+            collective_id=0, has_side_effects=True, vmem_limit_bytes=60 * 1024 * 1024
         ),
-    )(probes, leaf_basis, up_transfer, down_transfer, coupling, far_ids)
+    )(probes, leaf_basis.T, up_transfer, down_transfer, coupling, far_ids)
 
 
 def solution(mesh):

time: 26.5 us -> 19.9 us (0.75)
  local copies, waits for them, and re-layouts: 7.63 us -> 1.57 us
  Pallas kernels: 18.5 us -> 18.2 us
    unnamed x12 -> x1, local copies, waits for them, and re-layouts: 7.63 us -> 1.57 us
    pallas_call x1, Pallas kernels: 18.5 us -> 18.2 us  [shards(): pl.pallas_call(functools.partial(kernel, plan), out_shape=jax.ShapeDtypeS...]
where the time goes in v2:
time: 19.9 us; the launch traced here: 19.8 us
  Pallas kernels  18.2 us (91%)
  local copies, waits for them, and re-layouts  1.57 us (8%)
    pallas_call x1, Pallas kernels, shards(): pl.pallas_call(functools.partial(kernel, plan), out_shape=jax.ShapeDtypeS...  18.2 us
    unnamed x1, local copies, waits for them, and re-layouts  1.57 us

profile of v2, /device:TPU:1, one launch (start us, length us, event | category | flops | bytes accessed | tf_op | source)
XLA Modules:
  0.0 19.8 jit_solution(9986230799440297376)
XLA Ops:
  0.0 18.2 %shard_map.64 = bf16[2,8,32,128]{3,2,1,0:T(8,128)(2,1)} custom-call(bf16[2,8,32,128]{3,2,1,0:T(8,128)(2,1)} %probes.1, bf16[64,128]{1,0:T(8,128)(2,1)} %bitcast.1, bf16[7,4,64,64]{3,2,1,0:T(8,128)(2,1)} %up.1, bf16[7,4,64,64]{3,2,1,0:T(8,128)(2,1)} %down.1, bf16[8,40,64,64]{3,2,1,0:T(8,128)(2,1)} %coupling.1, s32[8,4,27]{2,1,0:T(4,128)} %ids_hbm.1), custom_call_target="tpu_custom_call" | custom-call | tf_op jit(solution)/shard_map/pallas_call | solution.py:445
  18.2 1.6 %copy.8 = bf16[2,8,32,128]{3,2,1,0:T(8,128)(2,1)} copy(bf16[2,8,32,128]{3,2,1,0:T(8,128)(2,1)} %shard_map.64) | data formatting | bytes 262144

commit v3 on v2

--- a/solution.py
+++ b/solution.py
@@ -53,12 +53,12 @@
 
 def kernel(
     plan, probes, basis, up, down, coupling, ids_hbm, out,
-    pbuf, s0, l1, l3, table, basisv, ids, basis2, upv, downv, updup, downst, *rest,
+    pbuf, s0, l1, l1side, s2, l3, table, basisv, ids, basis2, upv, downv, updup, downst, *rest,
 ):
     far_levels, top = plan.far_levels, plan.top
     weights, coup, rest = rest[:far_levels], rest[far_levels : 2 * far_levels], rest[2 * far_levels :]
     tops, rest = rest[: top - 2], rest[top - 2 :]
-    local_sem, send_sem, precv, crecv, l1recv, l3recv = rest
+    local_sem, send_sem, rowrecv, colrecv, cornerrecv, l1recv, siderecv, l3recv = rest
     rows_dev, cols_dev, quads, pad = plan.rows_dev, plan.cols_dev, plan.quads, plan.pad
     g = lax.axis_index("gx")
     y = lax.axis_index("gy")
@@ -68,22 +68,17 @@
     def inside(row, col):
         return (row >= 0) & (row < rows_dev) & (col >= 0) & (col < cols_dev)
 
-    near_partners = []
-    for dq in quad_steps:
-        for k in range(4):
-            for dy in (-1, 0, 1):
-                if (dq, k, dy) != (0, 0, 0):
-                    near_partners.append((dq, k, dy))
+    near_partners = [(dq, k) for dq in quad_steps for k in range(4) if (dq, k) != (0, 0)]
     far_partners = [(kq, ky) for kq in range(quads) for ky in range(cols_dev) if (kq, ky) != (0, 0)]
 
-    def near_device(dq, k, dy):
-        return (quad + dq) * 4 + (member + k) % 4, y + dy
+    def near_device(dq, k):
+        return (quad + dq) * 4 + (member + k) % 4, y
 
     def far_device(kq, ky):
         return (quad + kq) % quads * 4 + member, (y + ky) % cols_dev
 
     def met(row, col):
-        return (abs(row // 4 - quad) <= 1) & (abs(col - y) <= 1)
+        return (abs(row // 4 - quad) <= 1) & (col == y)
 
     barrier = pltpu.get_barrier_semaphore()
     expected = jnp.int32(0)
@@ -119,29 +114,45 @@
     for copy in fetch + fetch_coup:
         copy.start()
 
-    p_row_src = {0: slice(1, 3), 1: slice(2, 3), -1: slice(1, 2)}
-    p_row_dst = {0: slice(1, 3), 1: slice(0, 1), -1: slice(3, 4)}
-    p_col_src = {0: slice(1, 9), 1: slice(8, 9), -1: slice(1, 2)}
-    p_col_dst = {0: slice(1, 9), 1: slice(0, 1), -1: slice(9, 10)}
-    c_row_dst = {0: slice(1, 2), 1: slice(0, 1), -1: slice(2, 3)}
-    c_col_src = {0: slice(1, 5), 1: slice(4, 5), -1: slice(1, 2)}
-    c_col_dst = {0: slice(1, 5), 1: slice(0, 1), -1: slice(5, 6)}
-
-    for du, dv in AROUND:
-
-        @pl.when(jnp.logical_not(inside(g - du, y - dv)))
-        def _():
-            part = pbuf.at[p_row_dst[du], p_col_dst[dv]]
-            part[...] = jnp.zeros(part.shape, BF16)
-            part = s0.at[c_row_dst[du], c_col_dst[dv]]
-            part[...] = jnp.zeros(part.shape, BF16)
-
     def clear(part):
         part[...] = jnp.zeros(part.shape, BF16)
 
+    halo_row = {1: 0, -1: 2}
+    probe_row = {1: 0, -1: 3}
+    own_adjacent = {1: 2, -1: 1}
+    far_half = {1: slice(0, 128), -1: slice(128, 256)}
+    near_half = {1: slice(128, 256), -1: slice(0, 128)}
+    probe_side = {1: slice(0, 1), -1: slice(9, 10)}
+    coef_side = {1: slice(0, 1), -1: slice(5, 6)}
+    own_probe_edge = {1: slice(8, 9), -1: slice(1, 2)}
+    own_coef_edge = {1: slice(4, 5), -1: slice(1, 2)}
+    side_of = {1: 0, -1: 1}
+    signs = (1, -1)
+
+    def row_inside(row):
+        return (row >= 0) & (row < rows_dev)
+
+    def col_inside(col):
+        return (col >= 0) & (col < cols_dev)
+
+    for d in signs:
+
+        @pl.when(jnp.logical_not(row_inside(g - d)))
+        def _():
+            clear(pbuf.at[probe_row[d]])
+            clear(s0.at[halo_row[d]])
+
+        @pl.when(jnp.logical_not(col_inside(y - d)))
+        def _():
+            clear(pbuf.at[:, probe_side[d]])
+            clear(s0.at[:, coef_side[d]])
+            clear(l1side.at[:, side_of[d]])
+            clear(s2.at[:, 1 - d])
+
     if quads == 1:
-        clear(l1.at[0:pad])
-        clear(l1.at[pad + 4 : 2 * pad + 4])
+        for part in (l1, l1side):
+            clear(part.at[0:pad])
+            clear(part.at[pad + 4 : 2 * pad + 4])
     else:
 
         @pl.when(quad == 0)
@@ -151,14 +162,6 @@
         @pl.when(quad == quads - 1)
         def _():
             clear(l1.at[8:12])
-
-    @pl.when(y == 0)
-    def _():
-        clear(l1.at[:, 0])
-
-    @pl.when(y == cols_dev - 1)
-    def _():
-        clear(l1.at[:, 2])
 
     for level_top in tops:
         clear(level_top)
@@ -200,7 +203,7 @@
     for pc in (0, 1):
         first = lifted[64 * pc : 64 * pc + 32]
         second = lifted[64 * pc + 32 : 64 * pc + 64]
-        l1[own_row, 1, pc] = jnp.where(half32 == 0, first, second).astype(BF16)
+        l1[own_row, pc] = jnp.where(half32 == 0, first, second).astype(BF16)
 
     pl.semaphore_wait(barrier, expected)
 
@@ -227,49 +230,47 @@
         else:
             pl.when(valid)(copy.wait_recv)
 
-    ordered = sorted(near_partners, key=lambda t: (abs(t[2]), abs(t[0])))
-    for dq, k, dy in ordered:
-        device = near_device(dq, k, dy)
+    ordered = sorted(near_partners, key=lambda t: abs(t[0]))
+    for dq, k in ordered:
+        device = near_device(dq, k)
         row = pad - 4 * dq + member
-        valid = None if (dq, dy) == (0, 0) else inside(*device)
-        send(l1.at[own_row, 1], l1.at[row, 1 - dy], l1recv.at[row, 1 - dy], device, valid)
-    for i, (du, dv) in sorted(enumerate(AROUND), key=lambda t: abs(t[1][1])):
-        device = (g + du, y + dv)
-        valid = inside(*device)
-        send(s0.at[1:2, c_col_src[dv]], s0.at[c_row_dst[du], c_col_dst[dv]], crecv.at[i], device, valid)
+        valid = None if dq == 0 else inside(*device)
+        send(l1.at[own_row], l1.at[row], l1recv.at[row], device, valid)
+
+    pieces = [(slice(1, 3), slice(1, 2)), (slice(7, 9), slice(4, 5)), (slice(3, 7), slice(2, 4))]
+
+    def send_rows(piece):
+        probe_cols, coef_cols = pieces[piece]
+        for d in signs:
+            device, valid = (g + d, y), row_inside(g + d)
+            send(
+                s0.at[1, coef_cols, :, far_half[d]], s0.at[halo_row[d], coef_cols, :, far_half[d]],
+                rowrecv.at[piece, side_of[d], 0], device, valid,
+            )
+            send(
+                pbuf.at[own_adjacent[d], probe_cols], pbuf.at[probe_row[d], probe_cols],
+                rowrecv.at[piece, side_of[d], 1], device, valid,
+            )
+
+    def receive_rows(piece):
+        probe_cols, coef_cols = pieces[piece]
+        for d in signs:
+            valid = row_inside(g - d)
+            receive(s0.at[halo_row[d], coef_cols, :, far_half[d]], rowrecv.at[piece, side_of[d], 0], valid)
+            receive(pbuf.at[probe_row[d], probe_cols], rowrecv.at[piece, side_of[d], 1], valid)
+
+    send_rows(0)
+    send_rows(1)
+    for d in signs:
+        device, valid = (g, y + d), col_inside(y + d)
+        send(s0.at[1, own_coef_edge[d]], s0.at[1, coef_side[d]], colrecv.at[side_of[d], 0], device, valid)
         send(
-            pbuf.at[p_row_src[du], p_col_src[dv]], pbuf.at[p_row_dst[du], p_col_dst[dv]],
-            precv.at[i], device, valid,
+            pbuf.at[1:3, own_probe_edge[d]], pbuf.at[1:3, probe_side[d]], colrecv.at[side_of[d], 1], device, valid
         )
+    send_rows(2)
 
     for l in range(1, top):
         make_updup(l)
-
-    def receive_l1(wanted):
-        for dq, k, dy in ordered:
-            if wanted(dq, dy):
-                device = near_device(dq, k, dy)
-                row = pad + 4 * dq + (member + k) % 4
-                valid = None if (dq, dy) == (0, 0) else inside(*device)
-                receive(l1.at[row, 1 + dy], l1recv.at[row, 1 + dy], valid)
-
-    def level2(dq, side):
-        parts = []
-        for e in (0, 1):
-            for pc in (0, 1):
-                row = pad + 4 * dq + 2 * e
-                parts.append(jnp.concatenate([l1[row, side, pc], l1[row + 1, side, pc]], axis=1))
-        lift = dot(jnp.concatenate(parts, axis=0), updup[1, 0:256])
-        both = [jnp.where(half32 == 0, lift[64 * e : 64 * e + 32], lift[64 * e + 32 : 64 * e + 64]) for e in (0, 1)]
-        return jnp.concatenate(both, axis=1).astype(BF16)
-
-    receive_l1(lambda dq, dy: dq == 0 and dy == 0)
-    two = {(0, 0): level2(0, 1)}
-    lift = dot(two[0, 0], updup[2, 0:256])
-    l3[quad, y] = jnp.where(half32 == y % 2, lift, 0.0).astype(BF16)
-    for kq, ky in far_partners:
-        device = far_device(kq, ky)
-        send(l3.at[quad, y], l3.at[quad, y], l3recv.at[quad, y], device, None)
 
     point_q = lax.broadcasted_iota(jnp.int32, (128, 128), 0)
     point_p = lax.broadcasted_iota(jnp.int32, (128, 128), 1)
@@ -280,6 +281,63 @@
         dc = col_apart + float(v * LEAF_COLS)
         t = jnp.sqrt(3.0 * (dr * dr + dc * dc)) / LENGTH_SCALE
         table[128 * i : 128 * i + 128] = ((1.0 + t) * jnp.exp(-t)).astype(BF16)
+
+    for dq, k in ordered:
+        row = pad + 4 * dq + (member + k) % 4
+        receive(l1.at[row], l1recv.at[row], None if dq == 0 else inside(*near_device(dq, k)))
+    parts = []
+    for dq in quad_steps:
+        for e in (0, 1):
+            for pc in (0, 1):
+                row = pad + 4 * dq + 2 * e
+                parts.append(jnp.concatenate([l1[row, pc], l1[row + 1, pc]], axis=1))
+    lift = dot(jnp.concatenate(parts, axis=0), updup[1, 0:256])
+    for i, dq in enumerate(quad_steps):
+        both = []
+        for e in (0, 1):
+            at = 128 * i + 64 * e
+            both.append(jnp.where(half32 == 0, lift[at : at + 32], lift[at + 32 : at + 64]))
+        s2[i, 1] = jnp.concatenate(both, axis=1).astype(BF16)
+    lift = dot(s2[quad_steps.index(0), 1], updup[2, 0:256])
+    l3[quad, y] = jnp.where(half32 == y % 2, lift, 0.0).astype(BF16)
+    for kq, ky in far_partners:
+        device = far_device(kq, ky)
+        send(l3.at[quad, y], l3.at[quad, y], l3recv.at[quad, y], device, None)
+    rows_sent = slice(pad, pad + 4) if quads == 1 else slice(0, plan.window)
+    for d in signs:
+        device, valid = (g, y + d), col_inside(y + d)
+        send(l1.at[rows_sent, (1 + d) // 2], l1side.at[rows_sent, side_of[d]], siderecv.at[side_of[d], 0], device, valid)
+        send(s2.at[:, 1], s2.at[:, 1 - d], siderecv.at[side_of[d], 1], device, valid)
+
+    def adjacent(parents):
+        rows = [
+            jnp.concatenate([pbuf[probe_row[d], 2 * p - 1], pbuf[probe_row[d], 2 * p]], axis=1)
+            for d in signs
+            for p in parents
+        ]
+        coefs = lax.dot_general(
+            jnp.concatenate(rows, axis=0), basis2[...], (((1,), (1,)), ((), ())), preferred_element_type=F32
+        ).astype(BF16)
+        at = 0
+        for d in signs:
+            for p in parents:
+                s0[halo_row[d], p, :, near_half[d]] = coefs[at : at + 32]
+                at += 32
+
+    receive_rows(0)
+    receive_rows(1)
+    adjacent((1, 4))
+    for d in signs:
+        for v in signs:
+            device, valid = (g, y + v), row_inside(g - d) & col_inside(y + v)
+            send(
+                s0.at[halo_row[d], own_coef_edge[v]], s0.at[halo_row[d], coef_side[v]],
+                cornerrecv.at[side_of[d], side_of[v], 0], device, valid,
+            )
+            send(
+                pbuf.at[probe_row[d], own_probe_edge[v]], pbuf.at[probe_row[d], probe_side[v]],
+                cornerrecv.at[side_of[d], side_of[v], 1], device, valid,
+            )
 
     fetch[2].wait()
     for l in range(top):
@@ -303,30 +361,39 @@
                         c = 2 * se + sf
                         weights[l][i, 64 * c : 64 * c + 64, 128 * e : 128 * e + 128] = jnp.concatenate(pair, axis=1)
 
-    receive_l1(lambda dq, dy: not (dq == 0 and dy == 0))
+    for d in signs:
+        valid = col_inside(y - d)
+        receive(l1side.at[rows_sent, side_of[d]], siderecv.at[side_of[d], 0], valid)
+        receive(s2.at[:, 1 - d], siderecv.at[side_of[d], 1], valid)
+        receive(s0.at[1, coef_side[d]], colrecv.at[side_of[d], 0], valid)
+        receive(pbuf.at[1:3, probe_side[d]], colrecv.at[side_of[d], 1], valid)
+    for kq, ky in far_partners:
+        row, col = (quad + kq) % quads, (y + ky) % cols_dev
+        receive(l3.at[row, col], l3recv.at[row, col], None)
+    receive_rows(2)
+    for d in signs:
+        for v in signs:
+            valid = row_inside(g - d) & col_inside(y - v)
+            receive(s0.at[halo_row[d], coef_side[v]], cornerrecv.at[side_of[d], side_of[v], 0], valid)
+            receive(pbuf.at[probe_row[d], probe_side[v]], cornerrecv.at[side_of[d], side_of[v], 1], valid)
+    adjacent((2, 3))
+
     pair_row = pad + 2 * (member // 2)
     far1 = jnp.zeros((64, 256), F32)
     for dr in (-1, 0, 1):
         row = pair_row + 2 * dr
         tiles = [
-            jnp.concatenate([l1[row, side, pc], l1[row + 1, side, pc]], axis=1)
-            for side, pc in ((0, 1), (1, 0), (1, 1), (2, 0))
+            jnp.concatenate([ref[row, at], ref[row + 1, at]], axis=1)
+            for ref, at in ((l1side, 0), (l1, 0), (l1, 1), (l1side, 1))
         ]
         for dc in (-1, 0, 1):
             if (dr, dc) in plan.offsets[1]:
                 lhs = jnp.concatenate([tiles[1 + dc], tiles[2 + dc]], axis=0)
                 far1 = far1 + dot(lhs, weights[1][plan.offsets[1].index((dr, dc))])
-    for dq in quad_steps:
-        for dy in (-1, 0, 1):
-            if (dq, dy) != (0, 0):
-                two[dq, dy] = level2(dq, 1 + dy)
     far2 = jnp.zeros((32, 256), F32)
     for i, (dr, dc) in enumerate(plan.offsets[2]):
-        far2 = far2 + dot(two[dr, dc], weights[2][i])
-
-    for kq, ky in far_partners:
-        row, col = (quad + kq) % quads, (y + ky) % cols_dev
-        receive(l3.at[row, col], l3recv.at[row, col], None)
+        far2 = far2 + dot(s2[quad_steps.index(dr), 1 + dc], weights[2][i])
+
     for l in range(3, far_levels):
         pr_count, pc_count = plan.parents[l]
         level_top = tops[l - 3]
@@ -375,16 +442,12 @@
     ).astype(BF16)
     total = dot(local, downst[0])
 
-    for i, (du, dv) in enumerate(AROUND):
-        receive(s0.at[c_row_dst[du], c_col_dst[dv]], crecv.at[i], inside(g - du, y - dv))
     for i, (dr, dc) in enumerate(plan.offsets[0]):
         total = total + dot(s0[1 + dr, 1 + dc : 5 + dc].reshape(128, 256), weights[0][i])
     local = total.astype(BF16)
     local = jnp.concatenate([local[:, 0:128], local[:, 128:256]], axis=0)
     spread = dot(local, basis2[...])
 
-    for i, (du, dv) in enumerate(AROUND):
-        receive(pbuf.at[p_row_dst[du], p_col_dst[dv]], precv.at[i], inside(g - du, y - dv))
     for e in (0, 1):
         lhs = jnp.concatenate(
             [
@@ -410,12 +473,14 @@
 def shards(plan, probes, leaf_basis, up_transfer, down_transfer, coupling, far_ids):
     quads, cols_dev, far_levels, top = plan.quads, plan.cols_dev, plan.far_levels, plan.top
     dma = pltpu.SemaphoreType.DMA
-    near_count = 3 * 4 * (1 if quads == 1 else 3) - 1
-    send_count = near_count + 16 + quads * cols_dev - 1
+    near_count = 4 * (1 if quads == 1 else 3) - 1
+    send_count = near_count + 12 + 4 + quads * cols_dev - 1 + 4 + 8
     scratch = [
         pltpu.VMEM((4, 10, 32, 128), BF16),
         pltpu.VMEM((3, 6, 32, 256), BF16),
-        pltpu.VMEM((plan.window, 3, 2, 32, 128), BF16),
+        pltpu.VMEM((plan.window, 2, 32, 128), BF16),
+        pltpu.VMEM((plan.window, 2, 32, 128), BF16),
+        pltpu.VMEM((1 if quads == 1 else 3, 3, 32, 256), BF16),
         pltpu.VMEM((quads, cols_dev, 32, 128), BF16),
         pltpu.VMEM((9 * 128, 128), BF16),
         pltpu.VMEM((64, 128), BF16),
@@ -435,9 +500,11 @@
     scratch += [
         dma((5 + far_levels,)),
         dma((send_count,)),
-        dma((8,)),
-        dma((8,)),
-        dma((plan.window, 3)),
+        dma((3, 2, 2)),
+        dma((2, 2)),
+        dma((2, 2, 2)),
+        dma((plan.window,)),
+        dma((2, 2)),
         dma((quads, cols_dev)),
     ]
     anywhere = pl.BlockSpec(memory_space=pltpu.HBM)

time: 19.9 us -> 17.7 us (0.89)
  Pallas kernels: 18.2 us -> 15.9 us
    pallas_call x1, Pallas kernels: 18.2 us -> 15.9 us  [shards(): pl.pallas_call(functools.partial(kernel, plan), out_shape=jax.ShapeDtypeS...]
where the time goes in v3:
time: 17.7 us; the launch traced here: 17.5 us
  Pallas kernels  15.9 us (90%)
  local copies, waits for them, and re-layouts  1.57 us (9%)
    pallas_call x1, Pallas kernels, shards(): pl.pallas_call(functools.partial(kernel, plan), out_shape=jax.ShapeDtypeS...  15.9 us
    unnamed x1, local copies, waits for them, and re-layouts  1.57 us

profile of v3, /device:TPU:1, one launch (start us, length us, event | category | flops | bytes accessed | tf_op | source)
XLA Modules:
  0.0 17.5 jit_solution(5516023710650034643)
XLA Ops:
  0.0 15.9 %shard_map.64 = bf16[2,8,32,128]{3,2,1,0:T(8,128)(2,1)} custom-call(bf16[2,8,32,128]{3,2,1,0:T(8,128)(2,1)} %probes.1, bf16[64,128]{1,0:T(8,128)(2,1)} %bitcast.1, bf16[7,4,64,64]{3,2,1,0:T(8,128)(2,1)} %up.1, bf16[7,4,64,64]{3,2,1,0:T(8,128)(2,1)} %down.1, bf16[8,40,64,64]{3,2,1,0:T(8,128)(2,1)} %coupling.1, s32[8,4,27]{2,1,0:T(4,128)} %ids_hbm.1), custom_call_target="tpu_custom_call" | custom-call | tf_op jit(solution)/shard_map/pallas_call | solution.py:512
  15.9 1.6 %copy.8 = bf16[2,8,32,128]{3,2,1,0:T(8,128)(2,1)} copy(bf16[2,8,32,128]{3,2,1,0:T(8,128)(2,1)} %shard_map.64) | data formatting | bytes 262144

commit v4 on v3

--- a/solution.py
+++ b/solution.py
@@ -509,6 +509,10 @@
     ]
     anywhere = pl.BlockSpec(memory_space=pltpu.HBM)
     vmem = pl.BlockSpec(memory_space=pltpu.VMEM)
+    operands = [
+        pltpu.with_memory_space_constraint(x, pltpu.HBM)
+        for x in (probes, leaf_basis.T, up_transfer, down_transfer, coupling, far_ids)
+    ]
     return pl.pallas_call(
         functools.partial(kernel, plan),
         out_shape=jax.ShapeDtypeStruct(probes.shape, BF16),
@@ -516,9 +520,9 @@
         out_specs=vmem,
         scratch_shapes=scratch,
         compiler_params=pltpu.CompilerParams(
-            collective_id=0, has_side_effects=True, vmem_limit_bytes=60 * 1024 * 1024
+            collective_id=0, has_side_effects=True, vmem_limit_bytes=40 * 1024 * 1024
         ),
-    )(probes, leaf_basis.T, up_transfer, down_transfer, coupling, far_ids)
+    )(*operands)
 
 
 def solution(mesh):

time: 17.7 us -> 16.1 us (0.910)
  local copies, waits for them, and re-layouts: 1.57 us -> 0.66 us
  Pallas kernels: 15.9 us -> 15.3 us
    unnamed x1, local copies, waits for them, and re-layouts: 1.57 us -> 0.66 us
    pallas_call x1, Pallas kernels: 15.9 us -> 15.3 us  [shards(): pl.pallas_call(functools.partial(kernel, plan), out_shape=jax.ShapeDtypeS...]
where the time goes in v4:
time: 16.1 us; the launch traced here: 16 us
  Pallas kernels  15.3 us (95%)
  local copies, waits for them, and re-layouts  0.66 us (4%)
    pallas_call x1, Pallas kernels, shards(): pl.pallas_call(functools.partial(kernel, plan), out_shape=jax.ShapeDtypeS...  15.3 us
    unnamed x1, local copies, waits for them, and re-layouts  0.66 us

profile of v4, /device:TPU:1, one launch (start us, length us, event | category | flops | bytes accessed | tf_op | source)
XLA Modules:
  0.0 16.0 jit_solution(12240559327517958111)
XLA Ops:
  0.0 15.3 %shard_map.64 = bf16[2,8,32,128]{3,2,1,0:T(8,128)(2,1)S(1)} custom-call(bf16[2,8,32,128]{3,2,1,0:T(8,128)(2,1)} %probes.1, bf16[64,128]{1,0:T(8,128)(2,1)} %bitcast.1, bf16[7,4,64,64]{3,2,1,0:T(8,128)(2,1)} %up.1, bf16[7,4,64,64]{3,2,1,0:T(8,128)(2,1)} %down.1, bf16[8,40,64,64]{3,2,1,0:T(8,128)(2,1)} %coupling.1, s32[8,4,27]{2,1,0:T(4,128)} %ids_hbm.1), custom_call_target="tpu_custom_call" | custom-call | tf_op jit(solution)/shard_map/pallas_call | solution.py:516
  15.3 0.7 %copy.8 = bf16[2,8,32,128]{3,2,1,0:T(8,128)(2,1)} copy(bf16[2,8,32,128]{3,2,1,0:T(8,128)(2,1)S(1)} %shard_map.64) | data formatting | bytes 262144

commit v5 on v4

--- a/solution.py
+++ b/solution.py
@@ -111,7 +111,9 @@
     fetch_coup = [
         pltpu.make_async_copy(coupling.at[l], coup[l], local_sem.at[5 + l]) for l in range(far_levels)
     ]
-    for copy in fetch + fetch_coup:
+    for at in (3, 0, 1, 4, 2):
+        fetch[at].start()
+    for copy in reversed(fetch_coup):
         copy.start()
 
     def clear(part):
@@ -165,6 +167,16 @@
 
     for level_top in tops:
         clear(level_top)
+
+    point_q = lax.broadcasted_iota(jnp.int32, (128, 128), 0)
+    point_p = lax.broadcasted_iota(jnp.int32, (128, 128), 1)
+    row_apart = (point_q // LEAF_COLS - point_p // LEAF_COLS).astype(F32)
+    col_apart = (point_q % LEAF_COLS - point_p % LEAF_COLS).astype(F32)
+    for i, (u, v) in enumerate([(u, v) for u in (-1, 0, 1) for v in (-1, 0, 1)]):
+        dr = row_apart + float(u * LEAF_ROWS)
+        dc = col_apart + float(v * LEAF_COLS)
+        t = jnp.sqrt(3.0 * (dr * dr + dc * dc)) / LENGTH_SCALE
+        table[128 * i : 128 * i + 128] = ((1.0 + t) * jnp.exp(-t)).astype(BF16)
 
     basis2[...] = jnp.zeros((128, 256), BF16)
     fetch[3].wait()
@@ -208,83 +220,107 @@
     pl.semaphore_wait(barrier, expected)
 
     sent = []
-
-    def send(src, dst, recv, device, valid):
-        copy = pltpu.make_async_remote_copy(
-            src_ref=src, dst_ref=dst, send_sem=send_sem.at[len(sent)], recv_sem=recv,
-            device_id=device, device_id_type=MESH,
-        )
-        sent.append((copy, valid))
-        if valid is None:
-            copy.start()
-        else:
-            pl.when(valid)(copy.start)
-
-    def receive(dst, recv, valid):
-        copy = pltpu.make_async_remote_copy(
-            src_ref=dst, dst_ref=dst, send_sem=send_sem.at[0], recv_sem=recv,
-            device_id=(g, y), device_id_type=MESH,
-        )
-        if valid is None:
-            copy.wait_recv()
-        else:
-            pl.when(valid)(copy.wait_recv)
-
-    ordered = sorted(near_partners, key=lambda t: abs(t[0]))
-    for dq, k in ordered:
-        device = near_device(dq, k)
+    count = [0]
+
+    def send(valid, parts):
+        copies = []
+        for src, dst, recv, device in parts:
+            copies.append(
+                pltpu.make_async_remote_copy(
+                    src_ref=src, dst_ref=dst, send_sem=send_sem.at[count[0]], recv_sem=recv,
+                    device_id=device, device_id_type=MESH,
+                )
+            )
+            count[0] += 1
+        sent.append((valid, copies))
+
+        def start():
+            for copy in copies:
+                copy.start()
+
+        start() if valid is None else pl.when(valid)(start)
+
+    def receive(valid, parts):
+        def wait():
+            for dst, recv in parts:
+                pltpu.make_async_remote_copy(
+                    src_ref=dst, dst_ref=dst, send_sem=send_sem.at[0], recv_sem=recv,
+                    device_id=(g, y), device_id_type=MESH,
+                ).wait_recv()
+
+        wait() if valid is None else pl.when(valid)(wait)
+
+    def row_parts(d, piece):
+        probe_cols, coef_cols = pieces[piece]
+        return [
+            (
+                s0.at[1, coef_cols, :, far_half[d]], s0.at[halo_row[d], coef_cols, :, far_half[d]],
+                rowrecv.at[piece, side_of[d], 0], (g + d, y),
+            ),
+            (
+                pbuf.at[own_adjacent[d], probe_cols], pbuf.at[probe_row[d], probe_cols],
+                rowrecv.at[piece, side_of[d], 1], (g + d, y),
+            ),
+        ]
+
+    def arrivals(parts):
+        return [(dst, recv) for _, dst, recv, _ in parts]
+
+    for dq in sorted(quad_steps, key=abs):
+        valid = None if dq == 0 else (quad + dq >= 0) & (quad + dq < quads)
         row = pad - 4 * dq + member
-        valid = None if dq == 0 else inside(*device)
-        send(l1.at[own_row], l1.at[row], l1recv.at[row], device, valid)
+        send(valid, [
+            (l1.at[own_row], l1.at[row], l1recv.at[row], near_device(q, k)) for q, k in near_partners if q == dq
+        ])
 
     pieces = [(slice(1, 3), slice(1, 2)), (slice(7, 9), slice(4, 5)), (slice(3, 7), slice(2, 4))]
-
-    def send_rows(piece):
-        probe_cols, coef_cols = pieces[piece]
-        for d in signs:
-            device, valid = (g + d, y), row_inside(g + d)
-            send(
-                s0.at[1, coef_cols, :, far_half[d]], s0.at[halo_row[d], coef_cols, :, far_half[d]],
-                rowrecv.at[piece, side_of[d], 0], device, valid,
-            )
-            send(
-                pbuf.at[own_adjacent[d], probe_cols], pbuf.at[probe_row[d], probe_cols],
-                rowrecv.at[piece, side_of[d], 1], device, valid,
-            )
-
-    def receive_rows(piece):
-        probe_cols, coef_cols = pieces[piece]
-        for d in signs:
-            valid = row_inside(g - d)
-            receive(s0.at[halo_row[d], coef_cols, :, far_half[d]], rowrecv.at[piece, side_of[d], 0], valid)
-            receive(pbuf.at[probe_row[d], probe_cols], rowrecv.at[piece, side_of[d], 1], valid)
-
-    send_rows(0)
-    send_rows(1)
-    for d in signs:
-        device, valid = (g, y + d), col_inside(y + d)
-        send(s0.at[1, own_coef_edge[d]], s0.at[1, coef_side[d]], colrecv.at[side_of[d], 0], device, valid)
-        send(
-            pbuf.at[1:3, own_probe_edge[d]], pbuf.at[1:3, probe_side[d]], colrecv.at[side_of[d], 1], device, valid
-        )
-    send_rows(2)
+    for d in signs:
+        send(row_inside(g + d), row_parts(d, 0) + row_parts(d, 1))
+
+    def col_parts(d):
+        return [
+            (s0.at[1, own_coef_edge[d]], s0.at[1, coef_side[d]], colrecv.at[side_of[d], 0], (g, y + d)),
+            (pbuf.at[1:3, own_probe_edge[d]], pbuf.at[1:3, probe_side[d]], colrecv.at[side_of[d], 1], (g, y + d)),
+        ]
+
+    for d in signs:
+        send(col_inside(y + d), col_parts(d))
+    for d in signs:
+        send(row_inside(g + d), row_parts(d, 2))
 
     for l in range(1, top):
         make_updup(l)
 
-    point_q = lax.broadcasted_iota(jnp.int32, (128, 128), 0)
-    point_p = lax.broadcasted_iota(jnp.int32, (128, 128), 1)
-    row_apart = (point_q // LEAF_COLS - point_p // LEAF_COLS).astype(F32)
-    col_apart = (point_q % LEAF_COLS - point_p % LEAF_COLS).astype(F32)
-    for i, (u, v) in enumerate([(u, v) for u in (-1, 0, 1) for v in (-1, 0, 1)]):
-        dr = row_apart + float(u * LEAF_ROWS)
-        dc = col_apart + float(v * LEAF_COLS)
-        t = jnp.sqrt(3.0 * (dr * dr + dc * dc)) / LENGTH_SCALE
-        table[128 * i : 128 * i + 128] = ((1.0 + t) * jnp.exp(-t)).astype(BF16)
-
-    for dq, k in ordered:
-        row = pad + 4 * dq + (member + k) % 4
-        receive(l1.at[row], l1recv.at[row], None if dq == 0 else inside(*near_device(dq, k)))
+    fetch[2].wait()
+    for l in range(top):
+        for e in range(plan.ne[l]):
+            wide = jnp.concatenate([downv[l, 2 * e], downv[l, 2 * e + 1]], axis=1)
+            for c in range(2 * plan.ne[l + 1]):
+                downst[l, 64 * c : 64 * c + 64, 128 * e : 128 * e + 128] = wide
+
+    empty = jnp.zeros((64, 64), BF16)
+
+    def assemble(l):
+        fetch_coup[l].wait()
+        for i, (dr, dc) in enumerate(plan.offsets[l]):
+            for se in range(plan.ne[l]):
+                for sf in (0, 1):
+                    for e in range(plan.ne[l]):
+                        pair = []
+                        for f in (0, 1):
+                            slot = SLOT_OF[e, f].get((2 * dr + se - e, 2 * dc + sf - f))
+                            pair.append(empty if slot is None else coup[l][ids[l, 2 * e + f, slot]])
+                        c = 2 * se + sf
+                        weights[l][i, 64 * c : 64 * c + 64, 128 * e : 128 * e + 128] = jnp.concatenate(pair, axis=1)
+
+    fetch[4].wait()
+    for l in reversed(range(2, far_levels)):
+        assemble(l)
+
+    for dq in sorted(quad_steps, key=abs):
+        valid = None if dq == 0 else (quad + dq >= 0) & (quad + dq < quads)
+        rows = [pad + 4 * dq + (member + k) % 4 for q, k in near_partners if q == dq]
+        receive(valid, [(l1.at[row], l1recv.at[row]) for row in rows])
     parts = []
     for dq in quad_steps:
         for e in (0, 1):
@@ -300,14 +336,19 @@
         s2[i, 1] = jnp.concatenate(both, axis=1).astype(BF16)
     lift = dot(s2[quad_steps.index(0), 1], updup[2, 0:256])
     l3[quad, y] = jnp.where(half32 == y % 2, lift, 0.0).astype(BF16)
-    for kq, ky in far_partners:
-        device = far_device(kq, ky)
-        send(l3.at[quad, y], l3.at[quad, y], l3recv.at[quad, y], device, None)
+    send(None, [
+        (l3.at[quad, y], l3.at[quad, y], l3recv.at[quad, y], far_device(kq, ky)) for kq, ky in far_partners
+    ])
     rows_sent = slice(pad, pad + 4) if quads == 1 else slice(0, plan.window)
-    for d in signs:
-        device, valid = (g, y + d), col_inside(y + d)
-        send(l1.at[rows_sent, (1 + d) // 2], l1side.at[rows_sent, side_of[d]], siderecv.at[side_of[d], 0], device, valid)
-        send(s2.at[:, 1], s2.at[:, 1 - d], siderecv.at[side_of[d], 1], device, valid)
+
+    def side_parts(d):
+        return [
+            (l1.at[rows_sent, (1 + d) // 2], l1side.at[rows_sent, side_of[d]], siderecv.at[side_of[d], 0], (g, y + d)),
+            (s2.at[:, 1], s2.at[:, 1 - d], siderecv.at[side_of[d], 1], (g, y + d)),
+        ]
+
+    for d in signs:
+        send(col_inside(y + d), side_parts(d))
 
     def adjacent(parents):
         rows = [
@@ -324,58 +365,39 @@
                 s0[halo_row[d], p, :, near_half[d]] = coefs[at : at + 32]
                 at += 32
 
-    receive_rows(0)
-    receive_rows(1)
+    def corner_parts(d, v):
+        return [
+            (
+                s0.at[halo_row[d], own_coef_edge[v]], s0.at[halo_row[d], coef_side[v]],
+                cornerrecv.at[side_of[d], side_of[v], 0], (g, y + v),
+            ),
+            (
+                pbuf.at[probe_row[d], own_probe_edge[v]], pbuf.at[probe_row[d], probe_side[v]],
+                cornerrecv.at[side_of[d], side_of[v], 1], (g, y + v),
+            ),
+        ]
+
+    for d in signs:
+        receive(row_inside(g - d), arrivals(row_parts(d, 0) + row_parts(d, 1)))
     adjacent((1, 4))
     for d in signs:
         for v in signs:
-            device, valid = (g, y + v), row_inside(g - d) & col_inside(y + v)
-            send(
-                s0.at[halo_row[d], own_coef_edge[v]], s0.at[halo_row[d], coef_side[v]],
-                cornerrecv.at[side_of[d], side_of[v], 0], device, valid,
-            )
-            send(
-                pbuf.at[probe_row[d], own_probe_edge[v]], pbuf.at[probe_row[d], probe_side[v]],
-                cornerrecv.at[side_of[d], side_of[v], 1], device, valid,
-            )
-
-    fetch[2].wait()
-    for l in range(top):
-        for e in range(plan.ne[l]):
-            wide = jnp.concatenate([downv[l, 2 * e], downv[l, 2 * e + 1]], axis=1)
-            for c in range(2 * plan.ne[l + 1]):
-                downst[l, 64 * c : 64 * c + 64, 128 * e : 128 * e + 128] = wide
-
-    empty = jnp.zeros((64, 64), BF16)
-    fetch[4].wait()
-    for l in reversed(range(far_levels)):
-        fetch_coup[l].wait()
-        for i, (dr, dc) in enumerate(plan.offsets[l]):
-            for se in range(plan.ne[l]):
-                for sf in (0, 1):
-                    for e in range(plan.ne[l]):
-                        pair = []
-                        for f in (0, 1):
-                            slot = SLOT_OF[e, f].get((2 * dr + se - e, 2 * dc + sf - f))
-                            pair.append(empty if slot is None else coup[l][ids[l, 2 * e + f, slot]])
-                        c = 2 * se + sf
-                        weights[l][i, 64 * c : 64 * c + 64, 128 * e : 128 * e + 128] = jnp.concatenate(pair, axis=1)
-
-    for d in signs:
-        valid = col_inside(y - d)
-        receive(l1side.at[rows_sent, side_of[d]], siderecv.at[side_of[d], 0], valid)
-        receive(s2.at[:, 1 - d], siderecv.at[side_of[d], 1], valid)
-        receive(s0.at[1, coef_side[d]], colrecv.at[side_of[d], 0], valid)
-        receive(pbuf.at[1:3, probe_side[d]], colrecv.at[side_of[d], 1], valid)
-    for kq, ky in far_partners:
-        row, col = (quad + kq) % quads, (y + ky) % cols_dev
-        receive(l3.at[row, col], l3recv.at[row, col], None)
-    receive_rows(2)
+            send(row_inside(g - d) & col_inside(y + v), corner_parts(d, v))
+
+    assemble(1)
+    assemble(0)
+
+    receive(None, [
+        (l3.at[row, col], l3recv.at[row, col])
+        for row, col in [((quad + kq) % quads, (y + ky) % cols_dev) for kq, ky in far_partners]
+    ])
+    for d in signs:
+        receive(col_inside(y - d), arrivals(side_parts(d) + col_parts(d)))
+    for d in signs:
+        receive(row_inside(g - d), arrivals(row_parts(d, 2)))
     for d in signs:
         for v in signs:
-            valid = row_inside(g - d) & col_inside(y - v)
-            receive(s0.at[halo_row[d], coef_side[v]], cornerrecv.at[side_of[d], side_of[v], 0], valid)
-            receive(pbuf.at[probe_row[d], probe_side[v]], cornerrecv.at[side_of[d], side_of[v], 1], valid)
+            receive(row_inside(g - d) & col_inside(y - v), arrivals(corner_parts(d, v)))
     adjacent((2, 3))
 
     pair_row = pad + 2 * (member // 2)
@@ -463,11 +485,13 @@
             far = spread[128 * e + 32 * p : 128 * e + 32 * p + 32, 128 * f : 128 * f + 128]
             out[e, b] = (near[32 * b : 32 * b + 32] + far).astype(BF16)
 
-    for copy, valid in sent:
-        if valid is None:
-            copy.wait_send()
-        else:
-            pl.when(valid)(copy.wait_send)
+    for valid, copies in sent:
+
+        def finish():
+            for copy in copies:
+                copy.wait_send()
+
+        finish() if valid is None else pl.when(valid)(finish)
 
 
 def shards(plan, probes, leaf_basis, up_transfer, down_transfer, coupling, far_ids):

time: 16.1 us -> 16.2 us (level)
  no operation moved by 1% of the time
where the time goes in v5:
time: 16.2 us; the launch traced here: 16 us
  Pallas kernels  15.3 us (94%)
  local copies, waits for them, and re-layouts  0.66 us (4%)
    pallas_call x1, Pallas kernels, shards(): pl.pallas_call(functools.partial(kernel, plan), out_shape=jax.ShapeDtypeS...  15.3 us
    unnamed x1, local copies, waits for them, and re-layouts  0.66 us

profile of v5, /device:TPU:1, one launch (start us, length us, event | category | flops | bytes accessed | tf_op | source)
XLA Modules:
  0.0 16.0 jit_solution(16536452121059854439)
XLA Ops:
  0.0 15.3 %shard_map.64 = bf16[2,8,32,128]{3,2,1,0:T(8,128)(2,1)S(1)} custom-call(bf16[2,8,32,128]{3,2,1,0:T(8,128)(2,1)} %probes.1, bf16[64,128]{1,0:T(8,128)(2,1)} %bitcast.1, bf16[7,4,64,64]{3,2,1,0:T(8,128)(2,1)} %up.1, bf16[7,4,64,64]{3,2,1,0:T(8,128)(2,1)} %down.1, bf16[8,40,64,64]{3,2,1,0:T(8,128)(2,1)} %coupling.1, s32[8,4,27]{2,1,0:T(4,128)} %ids_hbm.1), custom_call_target="tpu_custom_call" | custom-call | tf_op jit(solution)/shard_map/pallas_call | solution.py:540
  15.3 0.7 %copy.8 = bf16[2,8,32,128]{3,2,1,0:T(8,128)(2,1)} copy(bf16[2,8,32,128]{3,2,1,0:T(8,128)(2,1)S(1)} %shard_map.64) | data formatting | bytes 262144

commit v6 on v5

--- a/solution.py
+++ b/solution.py
@@ -283,39 +283,9 @@
             (pbuf.at[1:3, own_probe_edge[d]], pbuf.at[1:3, probe_side[d]], colrecv.at[side_of[d], 1], (g, y + d)),
         ]
 
-    for d in signs:
-        send(col_inside(y + d), col_parts(d))
-    for d in signs:
-        send(row_inside(g + d), row_parts(d, 2))
 
     for l in range(1, top):
         make_updup(l)
-
-    fetch[2].wait()
-    for l in range(top):
-        for e in range(plan.ne[l]):
-            wide = jnp.concatenate([downv[l, 2 * e], downv[l, 2 * e + 1]], axis=1)
-            for c in range(2 * plan.ne[l + 1]):
-                downst[l, 64 * c : 64 * c + 64, 128 * e : 128 * e + 128] = wide
-
-    empty = jnp.zeros((64, 64), BF16)
-
-    def assemble(l):
-        fetch_coup[l].wait()
-        for i, (dr, dc) in enumerate(plan.offsets[l]):
-            for se in range(plan.ne[l]):
-                for sf in (0, 1):
-                    for e in range(plan.ne[l]):
-                        pair = []
-                        for f in (0, 1):
-                            slot = SLOT_OF[e, f].get((2 * dr + se - e, 2 * dc + sf - f))
-                            pair.append(empty if slot is None else coup[l][ids[l, 2 * e + f, slot]])
-                        c = 2 * se + sf
-                        weights[l][i, 64 * c : 64 * c + 64, 128 * e : 128 * e + 128] = jnp.concatenate(pair, axis=1)
-
-    fetch[4].wait()
-    for l in reversed(range(2, far_levels)):
-        assemble(l)
 
     for dq in sorted(quad_steps, key=abs):
         valid = None if dq == 0 else (quad + dq >= 0) & (quad + dq < quads)
@@ -348,7 +318,9 @@
         ]
 
     for d in signs:
-        send(col_inside(y + d), side_parts(d))
+        send(col_inside(y + d), side_parts(d) + col_parts(d))
+    for d in signs:
+        send(row_inside(g + d), row_parts(d, 2))
 
     def adjacent(parents):
         rows = [
@@ -383,6 +355,32 @@
     for d in signs:
         for v in signs:
             send(row_inside(g - d) & col_inside(y + v), corner_parts(d, v))
+
+    fetch[2].wait()
+    for l in range(top):
+        for e in range(plan.ne[l]):
+            wide = jnp.concatenate([downv[l, 2 * e], downv[l, 2 * e + 1]], axis=1)
+            for c in range(2 * plan.ne[l + 1]):
+                downst[l, 64 * c : 64 * c + 64, 128 * e : 128 * e + 128] = wide
+
+    empty = jnp.zeros((64, 64), BF16)
+
+    def assemble(l):
+        fetch_coup[l].wait()
+        for i, (dr, dc) in enumerate(plan.offsets[l]):
+            for se in range(plan.ne[l]):
+                for sf in (0, 1):
+                    for e in range(plan.ne[l]):
+                        pair = []
+                        for f in (0, 1):
+                            slot = SLOT_OF[e, f].get((2 * dr + se - e, 2 * dc + sf - f))
+                            pair.append(empty if slot is None else coup[l][ids[l, 2 * e + f, slot]])
+                        c = 2 * se + sf
+                        weights[l][i, 64 * c : 64 * c + 64, 128 * e : 128 * e + 128] = jnp.concatenate(pair, axis=1)
+
+    fetch[4].wait()
+    for l in reversed(range(2, far_levels)):
+        assemble(l)
 
     assemble(1)
     assemble(0)

time: 16.2 us -> 16.6 us (1.025)
  the two profiles are of different devices: /device:TPU:1 before, /device:TPU:0 now
where the time goes in v6:
time: 16.6 us; the launch traced here: 16.4 us
  Pallas kernels  15.7 us (95%)
  local copies, waits for them, and re-layouts  0.66 us (4%)
    pallas_call x1, Pallas kernels, shards(): pl.pallas_call(functools.partial(kernel, plan), out_shape=jax.ShapeDtypeS...  15.7 us
    unnamed x1, local copies, waits for them, and re-layouts  0.66 us

profile of v6, /device:TPU:0, one launch (start us, length us, event | category | flops | bytes accessed | tf_op | source)
XLA Modules:
  0.0 16.4 jit_solution(344607451171747832)
XLA Ops:
  0.0 15.7 %shard_map.64 = bf16[2,8,32,128]{3,2,1,0:T(8,128)(2,1)S(1)} custom-call(bf16[2,8,32,128]{3,2,1,0:T(8,128)(2,1)} %probes.1, bf16[64,128]{1,0:T(8,128)(2,1)} %bitcast.1, bf16[7,4,64,64]{3,2,1,0:T(8,128)(2,1)} %up.1, bf16[7,4,64,64]{3,2,1,0:T(8,128)(2,1)} %down.1, bf16[8,40,64,64]{3,2,1,0:T(8,128)(2,1)} %coupling.1, s32[8,4,27]{2,1,0:T(4,128)} %ids_hbm.1), custom_call_target="tpu_custom_call" | custom-call | tf_op jit(solution)/shard_map/pallas_call | solution.py:538
  15.7 0.7 %copy.8 = bf16[2,8,32,128]{3,2,1,0:T(8,128)(2,1)} copy(bf16[2,8,32,128]{3,2,1,0:T(8,128)(2,1)S(1)} %shard_map.64) | data formatting | bytes 262144

commit v7 on v5

--- a/solution.py
+++ b/solution.py
@@ -284,9 +284,9 @@
         ]
 
     for d in signs:
+        send(row_inside(g + d), row_parts(d, 2))
+    for d in signs:
         send(col_inside(y + d), col_parts(d))
-    for d in signs:
-        send(row_inside(g + d), row_parts(d, 2))
 
     for l in range(1, top):
         make_updup(l)
@@ -393,12 +393,6 @@
     ])
     for d in signs:
         receive(col_inside(y - d), arrivals(side_parts(d) + col_parts(d)))
-    for d in signs:
-        receive(row_inside(g - d), arrivals(row_parts(d, 2)))
-    for d in signs:
-        for v in signs:
-            receive(row_inside(g - d) & col_inside(y - v), arrivals(corner_parts(d, v)))
-    adjacent((2, 3))
 
     pair_row = pad + 2 * (member // 2)
     far1 = jnp.zeros((64, 256), F32)
@@ -464,22 +458,34 @@
     ).astype(BF16)
     total = dot(local, downst[0])
 
-    for i, (dr, dc) in enumerate(plan.offsets[0]):
-        total = total + dot(s0[1 + dr, 1 + dc : 5 + dc].reshape(128, 256), weights[0][i])
+    def far_leaf(total, rows):
+        for i, (dr, dc) in enumerate(plan.offsets[0]):
+            if dr in rows:
+                total = total + dot(s0[1 + dr, 1 + dc : 5 + dc].reshape(128, 256), weights[0][i])
+        return total
+
+    def near_rows(e, offs):
+        lhs = jnp.concatenate(
+            [pbuf[1 + e + u, 1 + v : 9 + v].reshape(256, 128) for u in offs for v in (-1, 0, 1)], axis=1
+        )
+        first = 384 * (offs[0] + 1)
+        return dot(lhs, table[first : first + 384 * len(offs)])
+
+    total = far_leaf(total, (0,))
+    near_own = [near_rows(e, (-e, 1 - e)) for e in (0, 1)]
+
+    for d in signs:
+        receive(row_inside(g - d), arrivals(row_parts(d, 2)))
+    for d in signs:
+        for v in signs:
+            receive(row_inside(g - d) & col_inside(y - v), arrivals(corner_parts(d, v)))
+    adjacent((2, 3))
+    total = far_leaf(total, (-1, 1))
     local = total.astype(BF16)
     local = jnp.concatenate([local[:, 0:128], local[:, 128:256]], axis=0)
     spread = dot(local, basis2[...])
-
     for e in (0, 1):
-        lhs = jnp.concatenate(
-            [
-                pbuf[1 + e + u, 1 + v : 9 + v].reshape(256, 128)
-                for u in (-1, 0, 1)
-                for v in (-1, 0, 1)
-            ],
-            axis=1,
-        )
-        near = dot(lhs, table[...])
+        near = near_own[e] + near_rows(e, (2 * e - 1,))
         for b in range(8):
             p, f = b // 2, b % 2
             far = spread[128 * e + 32 * p : 128 * e + 32 * p + 32, 128 * f : 128 * f + 128]

time: 16.2 us -> 16.3 us (level)
  the two profiles are of different devices: /device:TPU:1 before, /device:TPU:0 now
where the time goes in v7:
time: 16.3 us; the launch traced here: 16.1 us
  Pallas kernels  15.4 us (94%)
  local copies, waits for them, and re-layouts  0.66 us (4%)
    pallas_call x1, Pallas kernels, shards(): pl.pallas_call(functools.partial(kernel, plan), out_shape=jax.ShapeDtypeS...  15.4 us
    unnamed x1, local copies, waits for them, and re-layouts  0.66 us

profile of v7, /device:TPU:0, one launch (start us, length us, event | category | flops | bytes accessed | tf_op | source)
XLA Modules:
  0.0 16.1 jit_solution(16831763878300140862)
XLA Ops:
  0.0 15.4 %shard_map.64 = bf16[2,8,32,128]{3,2,1,0:T(8,128)(2,1)S(1)} custom-call(bf16[2,8,32,128]{3,2,1,0:T(8,128)(2,1)} %probes.1, bf16[64,128]{1,0:T(8,128)(2,1)} %bitcast.1, bf16[7,4,64,64]{3,2,1,0:T(8,128)(2,1)} %up.1, bf16[7,4,64,64]{3,2,1,0:T(8,128)(2,1)} %down.1, bf16[8,40,64,64]{3,2,1,0:T(8,128)(2,1)} %coupling.1, s32[8,4,27]{2,1,0:T(4,128)} %ids_hbm.1), custom_call_target="tpu_custom_call" | custom-call | tf_op jit(solution)/shard_map/pallas_call | solution.py:546
  15.4 0.7 %copy.8 = bf16[2,8,32,128]{3,2,1,0:T(8,128)(2,1)} copy(bf16[2,8,32,128]{3,2,1,0:T(8,128)(2,1)S(1)} %shard_map.64) | data formatting | bytes 262144

commit v8 on v5

--- a/solution.py
+++ b/solution.py
@@ -113,8 +113,6 @@
     ]
     for at in (3, 0, 1, 4, 2):
         fetch[at].start()
-    for copy in reversed(fetch_coup):
-        copy.start()
 
     def clear(part):
         part[...] = jnp.zeros(part.shape, BF16)
@@ -167,16 +165,6 @@
 
     for level_top in tops:
         clear(level_top)
-
-    point_q = lax.broadcasted_iota(jnp.int32, (128, 128), 0)
-    point_p = lax.broadcasted_iota(jnp.int32, (128, 128), 1)
-    row_apart = (point_q // LEAF_COLS - point_p // LEAF_COLS).astype(F32)
-    col_apart = (point_q % LEAF_COLS - point_p % LEAF_COLS).astype(F32)
-    for i, (u, v) in enumerate([(u, v) for u in (-1, 0, 1) for v in (-1, 0, 1)]):
-        dr = row_apart + float(u * LEAF_ROWS)
-        dc = col_apart + float(v * LEAF_COLS)
-        t = jnp.sqrt(3.0 * (dr * dr + dc * dc)) / LENGTH_SCALE
-        table[128 * i : 128 * i + 128] = ((1.0 + t) * jnp.exp(-t)).astype(BF16)
 
     basis2[...] = jnp.zeros((128, 256), BF16)
     fetch[3].wait()
@@ -284,12 +272,24 @@
         ]
 
     for d in signs:
+        send(row_inside(g + d), row_parts(d, 2))
+    for copy in reversed(fetch_coup):
+        copy.start()
+    for d in signs:
         send(col_inside(y + d), col_parts(d))
-    for d in signs:
-        send(row_inside(g + d), row_parts(d, 2))
 
     for l in range(1, top):
         make_updup(l)
+
+    point_q = lax.broadcasted_iota(jnp.int32, (128, 128), 0)
+    point_p = lax.broadcasted_iota(jnp.int32, (128, 128), 1)
+    row_apart = (point_q // LEAF_COLS - point_p // LEAF_COLS).astype(F32)
+    col_apart = (point_q % LEAF_COLS - point_p % LEAF_COLS).astype(F32)
+    for i, (u, v) in enumerate([(u, v) for u in (-1, 0, 1) for v in (-1, 0, 1)]):
+        dr = row_apart + float(u * LEAF_ROWS)
+        dc = col_apart + float(v * LEAF_COLS)
+        t = jnp.sqrt(3.0 * (dr * dr + dc * dc)) / LENGTH_SCALE
+        table[128 * i : 128 * i + 128] = ((1.0 + t) * jnp.exp(-t)).astype(BF16)
 
     fetch[2].wait()
     for l in range(top):

time: 16.2 us -> 16.2 us (level)
  no operation moved by 1% of the time
where the time goes in v8:
time: 16.2 us; the launch traced here: 16 us
  Pallas kernels  15.3 us (94%)
  local copies, waits for them, and re-layouts  0.66 us (4%)
    pallas_call x1, Pallas kernels, shards(): pl.pallas_call(functools.partial(kernel, plan), out_shape=jax.ShapeDtypeS...  15.3 us
    unnamed x1, local copies, waits for them, and re-layouts  0.66 us

profile of v8, /device:TPU:1, one launch (start us, length us, event | category | flops | bytes accessed | tf_op | source)
XLA Modules:
  0.0 16.0 jit_solution(315896306215314781)
XLA Ops:
  0.0 15.3 %shard_map.64 = bf16[2,8,32,128]{3,2,1,0:T(8,128)(2,1)S(1)} custom-call(bf16[2,8,32,128]{3,2,1,0:T(8,128)(2,1)} %probes.1, bf16[64,128]{1,0:T(8,128)(2,1)} %bitcast.1, bf16[7,4,64,64]{3,2,1,0:T(8,128)(2,1)} %up.1, bf16[7,4,64,64]{3,2,1,0:T(8,128)(2,1)} %down.1, bf16[8,40,64,64]{3,2,1,0:T(8,128)(2,1)} %coupling.1, s32[8,4,27]{2,1,0:T(4,128)} %ids_hbm.1), custom_call_target="tpu_custom_call" | custom-call | tf_op jit(solution)/shard_map/pallas_call | solution.py:540
  15.3 0.7 %copy.8 = bf16[2,8,32,128]{3,2,1,0:T(8,128)(2,1)} copy(bf16[2,8,32,128]{3,2,1,0:T(8,128)(2,1)S(1)} %shard_map.64) | data formatting | bytes 262144
